TPU v7x, 512 devices: a whole 4x8x8 slice. The times are simulated.
512 devices in a mesh: blk: 64 (over z_hi, y, core), rel: 8 (over z_lo, x).
Axes of the slice: x: 4, y: 8, z: 8 (z_hi: 4, z_lo: 2; z = z_hi * 2 + z_lo), core: 2. Of those that a mesh axis runs over, the one named last changes fastest.
Arguments:
- source_table: float32 [400, 393216], P(None, ('blk', 'rel')), may hold values from -1.2 to 1.2
- source_state: float32 [393216], P(('blk', 'rel')), may hold values from 0.001 to 0.1
- target_table: float32 [400, 393216], P(None, ('blk', 'rel')), may hold values from -1.2 to 1.2
- target_state: float32 [393216], P(('blk', 'rel')), may hold values from 0.001 to 0.1
- relation_ops: float32 [400, 8192], P(None, 'blk'), may hold values from 0.5 to 1.5
- relation_state: float32 [400, 8192], P(None, 'blk'), may hold values from 0.01 to 1
- source_ids: int32 [2, 262144], P(None, ('blk', 'rel')), may hold values from 0 to 767
- target_ids: int32 [2, 262144], P(None, ('blk', 'rel')), may hold values from 0 to 767
- relation_ids: int32 [2, 262144], P(None, ('blk', 'rel')), may hold values from 0 to 127
- negative_ids: int32 [2, 262144], P(None, ('blk', 'rel')), may hold values from 0 to 767
Outputs:
- new_source: float32 [400, 393216], P(None, ('blk', 'rel'))
- new_source_state: float32 [393216], P(('blk', 'rel'))
- held_target: float32 [400, 393216], P(None, ('blk', 'rel'))
- held_target_state: float32 [393216], P(('blk', 'rel'))
- new_relations: float32 [400, 8192], P(None, 'blk')
- new_relation_state: float32 [400, 8192], P(None, 'blk')
All inputs are finite; a program needn't handle non-finite values.
Results may differ from a plain program's by a relative error of at most 0.0001.
Values sent between devices are 32-bit elements; how exact they have to be, the bound alone decides.
No kernel may reach another device: no remote copies, remote signals or barrier semaphores. Data moves between devices by JAX's collectives and lax.ppermute only.
A program may use at most 64 MiB of HBM per device.

v0:
```python
import jax
import jax.numpy as jnp
from jax import lax
from jax.sharding import PartitionSpec as P

learn_rate = 0.1
epsilon = 1e-06
HIGHEST = lax.Precision.HIGHEST


def passed_along(value, axis, steps):
    count = lax.axis_size(axis)
    pairs = [(source, (source + steps) % count) for source in range(count)]
    return lax.ppermute(value, axis, pairs)


def sent_to_all(x, axis):
    devices = lax.axis_size(axis)
    return lax.all_to_all(jnp.broadcast_to(x[None], (devices, *x.shape)), axis, 0, 0, tiled=True)


def taken_together(x, axis):
    return sent_to_all(x, axis).sum(axis=0)


def one_hot(labels, length):
    return (
        lax.broadcasted_iota(jnp.int32, (length, labels.shape[0]), 0) == labels[None, :]
    ).astype(jnp.float32)


def pick_columns(matrix, selector):
    return jnp.dot(matrix, selector, precision=HIGHEST)


def add_columns(values, selector):
    return lax.dot_general(values, selector, (((1,), (1,)), ((), ())), precision=HIGHEST)


def row_adagrad(matrix, row_state, gradient):
    fresh = row_state + jnp.mean(gradient * gradient, axis=0)
    return (matrix - learn_rate * gradient / (jnp.sqrt(fresh) + epsilon)[None, :], fresh)


def bucket_terms(
    source_side, target_side, relations, source_idx, target_idx, relation_idx, negative_idx
):
    row_total = source_side.shape[1]
    edge_total = source_idx.shape[0]
    neg_total = negative_idx.shape[0]
    source_hot = one_hot(source_idx, row_total)
    target_hot = one_hot(jnp.concatenate([target_idx, negative_idx]), row_total)
    relation_hot = one_hot(relation_idx, relations.shape[1])
    source = pick_columns(source_side, source_hot)
    picked = pick_columns(target_side, target_hot)
    target = picked[:, :edge_total]
    negative = picked[:, edge_total:]
    relation = pick_columns(relations, relation_hot)
    queries = source * relation
    positive = jnp.sum(queries * target, axis=0)
    neg_score = lax.dot_general(queries, negative, (((0,), (0,)), ((), ())), precision=HIGHEST)
    pos_coef = -jax.nn.sigmoid(-positive)
    neg_coef = jax.nn.sigmoid(neg_score) / neg_total
    grad_query = target * pos_coef[None, :] + lax.dot_general(
        negative, neg_coef, (((1,), (1,)), ((), ())), precision=HIGHEST
    )
    grad_target = queries * pos_coef[None, :]
    grad_negative = jnp.dot(queries, neg_coef, precision=HIGHEST)
    target_grad = add_columns(jnp.concatenate([grad_target, grad_negative], axis=1), target_hot)
    relation_grad = add_columns(grad_query * source, relation_hot)
    return (target_grad, grad_query * relation, source_hot, relation_grad)


def per_device(
    source_table,
    source_state,
    target_table,
    target_state,
    relation_ops,
    relation_state,
    source_ids,
    target_ids,
    relation_ids,
    negative_ids,
):
    bucket_count = source_ids.shape[0]
    source_side, source_rows = (source_table, source_state)
    target_side, target_rows = (target_table, target_state)
    collected = []
    for bucket in range(bucket_count):
        target_grad, query_grad, source_hot, relation_grad = bucket_terms(
            source_side,
            target_side,
            relation_ops,
            source_ids[bucket],
            target_ids[bucket],
            relation_ids[bucket],
            negative_ids[bucket],
        )
        last = bucket + 1 >= bucket_count
        target_side, target_rows = row_adagrad(target_side, target_rows, target_grad)
        if not last:
            target_side, target_rows = passed_along((target_side, target_rows), "blk", 1)
        source_side, source_rows = row_adagrad(
            source_side, source_rows, add_columns(query_grad, source_hot)
        )
        collected.append(relation_grad)
    summed = collected[0]
    for extra_grad in collected[1:]:
        summed = summed + extra_grad
    summed = taken_together(summed, "rel")
    new_relation_state = relation_state + summed * summed
    new_relations = relation_ops - learn_rate * summed / (jnp.sqrt(new_relation_state) + epsilon)
    return (source_side, source_rows, target_side, target_rows, new_relations, new_relation_state)


def solution(mesh):
    placed = (
        P(None, ("blk", "rel")),
        P(("blk", "rel")),
        P(None, ("blk", "rel")),
        P(("blk", "rel")),
        P(None, "blk"),
        P(None, "blk"),
        P(None, ("blk", "rel")),
        P(None, ("blk", "rel")),
        P(None, ("blk", "rel")),
        P(None, ("blk", "rel")),
    )
    return jax.shard_map(
        per_device,
        mesh=mesh,
        in_specs=placed,
        out_specs=(
            P(None, ("blk", "rel")),
            P(("blk", "rel")),
            P(None, ("blk", "rel")),
            P(("blk", "rel")),
            P(None, "blk"),
            P(None, "blk"),
        ),
        check_vma=False,
    )
```

profile of v0, /device:TPU:2, one launch (start us, length us, event | category | flops | bytes accessed | tf_op | source)
XLA Modules:
  0.0 89.1 jit_solution(9452869631970758774)
XLA Ops:
  0.6 0.8 fusion.51
  1.4 0.8 fusion.52
  2.2 0.8 fusion.50
  2.9 0.8 fusion.53
  3.7 1.4 %convolution_bitcast_fusion.1 = f32[400,512]{1,0:T(8,128)S(1)} fusion(f32[400,128]{1,0:T(8,128)} %param.14, s32[512]{0:T(512)S(1)} %bitcast.33), kind=kOutput, calls=%fused_computation.36 | convolution fusion | flops 314638336 | bytes 1026048 | tf_op jit(solution)/shard_map/dot_general | solution.py:33
  5.2 0.0 copy-start
  5.2 3.6 %fusion.18 = f32[400,1024]{1,0:T(8,128)S(1)} fusion(f32[400,768]{1,0:T(8,128)} %param.12, s32[1024]{0:T(1024)S(1)} %pad_add_fusion), kind=kOutput, calls=%fused_computation.22 | convolution fusion | flops 3775660032 | bytes 2871296 | tf_op jit(solution)/shard_map/dot_general | solution.py:33
  8.8 0.0 copy-done
  8.8 1.3 %multiply_reduce_fusion.5 = (f32[512]{0:T(512)S(1)}, f32[400,512]{1,0:T(8,128)S(1)}, f32[400,512]{1,0:T(8,128)S(1)}) fusion(f32[400,1024]{1,0:T(8,128)S(1)} %fusion.18, f32[400,512]{1,0:T(8,128)S(1)} %convolution_bitcast_fusion.1, f32[400,768]{1,0:T(8,128)S(1)} %copy-done, s32[512]{0:T(512)S(1)} %bitcast.29), kind=kOutput, calls=%fused_computation.53 | convolution fusion | flops 1888443904 | bytes 4509696 | tf_op jit(solution)/shard_map/dot_general | solution.py:33
  10.1 2.1 %fusion.26 = f32[512,512]{1,0:T(8,128)S(1)} fusion(f32[400,512]{1,0:T(8,128)S(1)} %get-tuple-element.17, f32[400,1024]{1,0:T(8,128)S(1)} %fusion.18), kind=kOutput, calls=%fused_computation.32 | convolution fusion | flops 1259339776 | bytes 2686976 | tf_op jit(solution)/shard_map/dot_general | solution.py:61
  12.2 0.1 broadcast_multiply_fusion.1
  12.3 1.5 %fusion.54 = f32[400,512]{1,0:T(8,128)S(1)} fusion(f32[400,512]{1,0:T(8,128)S(1)} %get-tuple-element.17, f32[512,512]{1,0:T(8,128)S(1)} %fusion.26), kind=kOutput, calls=%fused_computation.91 | convolution fusion | flops 1258291200 | bytes 2686976 | tf_op jit(solution)/shard_map/dot_general | solution.py:68
  13.8 0.0 copy-start.15
  13.8 0.0 copy-start.10
  13.8 2.4 %multiply_reduce_fusion.2 = (f32[768]{0:T(1024)S(1)}, f32[400,768]{1,0:T(8,128)S(1)}) fusion(s32[1024]{0:T(1024)S(1)} %pad_add_fusion, f32[400,512]{1,0:T(8,128)S(1)} %fusion.54, f32[400,512]{1,0:T(8,128)S(1)} %broadcast_multiply_fusion.1), kind=kOutput, calls=%fused_computation.42 | convolution fusion | flops 3776683264 | bytes 2874368 | tf_op jit(solution)/shard_map/dot_general | solution.py:37
  16.3 0.0 copy-done.15
  16.3 0.0 copy-done.10
  16.3 0.2 divide_subtract_fusion.2
  16.5 2.1 %collective-permute-start = (f32[400,768]{1,0:T(8,128)S(1)}, f32[400,768]{1,0:T(8,128)S(1)}, u32[]{:S(2)}, u32[]{:S(2)}) collective-permute-start(f32[400,768]{1,0:T(8,128)S(1)} %divide_subtract_fusion.2), channel_id=1, source_target_pairs={{0,8},{8,16},{16,24},{24,32},{32,40},{40,48},{48,56},{56,64},{64,7... | collective-permute-start | bytes 3686408 | tf_op jit(solution)/shard_map/ppermute | solution.py:14
  18.6 1.5 %convolution_add_fusion = f32[400,512]{1,0:T(8,128)S(1)} fusion(f32[512,512]{1,0:T(8,128)S(1)} %fusion.26, f32[400,1024]{1,0:T(8,128)S(1)} %fusion.18, f32[512]{0:T(512)S(1)} %divide_negate_fusion.1), kind=kOutput, calls=%fused_computation.34 | convolution fusion | flops 1258700800 | bytes 3508224 | tf_op jit(solution)/shard_map/dot_general | solution.py:64
  20.1 0.0 copy-start.14
  20.1 0.0 copy-start.8
  20.1 1.4 %multiply_reduce_fusion.3 = (f32[768]{0:T(1024)S(1)}, f32[400,768]{1,0:T(8,128)S(1)}) fusion(s32[512]{0:T(512)S(1)} %bitcast.30, f32[400,512]{1,0:T(8,128)S(1)} %convolution_add_fusion, f32[400,512]{1,0:T(8,128)S(1)} %convolution_bitcast_fusion.1), kind=kOutput, calls=%fused_computation.44 | convolution fusion | flops 1888648448 | bytes 2872320 | tf_op jit(solution)/shard_map/dot_general | solution.py:37
  21.5 0.0 copy-start.2
  21.5 0.0 copy-done.14
  21.6 0.0 copy-done.8
  21.6 0.5 convolution_bitcast_fusion
  22.1 0.0 copy-start.4
  22.1 0.6 fusion.29
  22.6 34.7 %collective-permute-done = f32[400,768]{1,0:T(8,128)S(1)} collective-permute-done((f32[400,768]{1,0:T(8,128)S(1)}, f32[400,768]{1,0:T(8,128)S(1)}, u32[]{:S(2)}, u32[]{:S(2)}) %collective-permute-start) | collective-permute-done | bytes 1228832 | tf_op jit(solution)/shard_map/ppermute | solution.py:14
  57.3 2.3 %fusion.1 = f32[400,1024]{1,0:T(8,128)S(1)} fusion(f32[400,768]{1,0:T(8,128)S(1)} %collective-permute-done, s32[1024]{0:T(1024)S(1)} %pad_add_fusion.1), kind=kOutput, calls=%fused_computation.2 | convolution fusion | flops 3775660032 | bytes 2871296 | tf_op jit(solution)/shard_map/dot_general | solution.py:33
  59.6 0.0 copy-done.11
  59.7 0.0 copy-done.2
  59.7 0.0 copy-done.4
  59.7 1.4 %multiply_reduce_fusion.4 = (f32[512]{0:T(512)S(1)}, f32[400,512]{1,0:T(8,128)S(1)}, f32[400,512]{1,0:T(8,128)S(1)}) fusion(f32[400,1024]{1,0:T(8,128)S(1)} %fusion.1, f32[400,512]{1,0:T(8,128)S(1)} %convolution_bitcast_fusion, s32[512]{0:T(512)S(1)} %bitcast.35, f32[400,768]{1,0:T(8,128)S(1)} %copy-done, f32[400,768]{1,0:T(8,128)S(1)} %get-tuple-element.30, ...), kind=kOutput, calls=%fused_computation.51 | convolution fusion | flops 1889365504 | bytes 5741568 | tf_op jit(solution)/shard_map/dot_general | solution.py:33
  61.1 0.0 copy-start.6
  61.1 2.1 %fusion.22 = f32[512,512]{1,0:T(8,128)S(1)} fusion(f32[400,512]{1,0:T(8,128)S(1)} %get-tuple-element.13, f32[400,1024]{1,0:T(8,128)S(1)} %fusion.1), kind=kOutput, calls=%fused_computation.27 | convolution fusion | flops 1259339776 | bytes 2686976 | tf_op jit(solution)/shard_map/dot_general | solution.py:61
  63.2 0.0 copy-done.6
  63.2 1.5 %multiply_add_fusion = f32[400,512]{1,0:T(8,128)S(1)} fusion(f32[512,512]{1,0:T(8,128)S(1)} %fusion.22, f32[400,1024]{1,0:T(8,128)S(1)} %fusion.1, f32[512]{0:T(512)S(1)} %divide_negate_fusion), kind=kOutput, calls=%fused_computation.50 | convolution fusion | flops 1258700800 | bytes 3508224 | tf_op jit(solution)/shard_map/dot_general | solution.py:64
  64.7 0.6 convolution_add_fusion.1
  65.3 1.3 %broadcast_in_dim.2 = f32[8,400,128]{2,1,0:T(8,128)} broadcast(f32[400,128]{1,0:T(8,128)S(1)} %convolution_add_fusion.1), dimensions={1,2} | broadcast | bytes 1843200 | tf_op jit(solution)/shard_map/broadcast_in_dim | solution.py:19
  66.6 5.3 %all-to-all-start = ((f32[8,400,128]{2,1,0:T(8,128)}), f32[8,400,128]{2,1,0:T(8,128)S(1)}, u32[]{:S(2)}, u32[]{:S(2)}) async-start(f32[8,400,128]{2,1,0:T(8,128)} %broadcast_in_dim.2), calls=%async_computation | async-start | bytes 3276800 | tf_op jit(solution)/shard_map/all_to_all | solution.py:19
  71.9 0.0 copy-start.7
  71.9 2.3 %collective-permute-start.1 = (f32[768]{0:T(1024)S(1)}, f32[768]{0:T(1024)S(1)}, u32[]{:S(2)}, u32[]{:S(2)}) collective-permute-start(f32[768]{0:T(1024)S(1)} %get-tuple-element.15), channel_id=1, source_target_pairs={{0,8},{8,16},{16,24},{24,32},{32,40},{40,48},{48,56},{56,64},{64,7... | collective-permute-start | bytes 9224 | tf_op jit(solution)/shard_map/ppermute | solution.py:14
  74.1 1.2 %broadcast_multiply_fusion = f32[400,512]{1,0:T(8,128)S(1)} fusion(f32[400,512]{1,0:T(8,128)} %copy-done.6, f32[512]{0:T(512)S(1)} %divide_negate_fusion), kind=kLoop, calls=%fused_computation.63 | loop fusion | flops 204800 | bytes 1640448 | tf_op jit(solution)/shard_map/mul | solution.py:67
  75.4 0.0 copy-done.7
  75.4 1.5 %fusion.55 = f32[400,512]{1,0:T(8,128)S(1)} fusion(f32[400,512]{1,0:T(8,128)S(1)} %copy-done.7, f32[512,512]{1,0:T(8,128)S(1)} %fusion.22), kind=kOutput, calls=%fused_computation.92 | convolution fusion | flops 1258291200 | bytes 2686976 | tf_op jit(solution)/shard_map/dot_general | solution.py:68
  76.9 0.0 copy-start.5
  76.9 2.4 %multiply_reduce_fusion = (f32[768]{0:T(1024)S(1)}, f32[400,768]{1,0:T(8,128)S(1)}) fusion(s32[1024]{0:T(1024)S(1)} %pad_add_fusion.1, f32[400,512]{1,0:T(8,128)S(1)} %fusion.55, f32[400,512]{1,0:T(8,128)S(1)} %broadcast_multiply_fusion), kind=kOutput, calls=%fused_computation.38 | convolution fusion | flops 3776683264 | bytes 2874368 | tf_op jit(solution)/shard_map/dot_general | solution.py:37
  79.3 1.9 %collective-permute-done.1 = f32[768]{0:T(1024)S(1)} collective-permute-done((f32[768]{0:T(1024)S(1)}, f32[768]{0:T(1024)S(1)}, u32[]{:S(2)}, u32[]{:S(2)}) %collective-permute-start.1) | collective-permute-done | bytes 3104 | tf_op jit(solution)/shard_map/ppermute | solution.py:14
  81.2 0.6 sqrt_add_fusion
  81.8 0.0 copy-done.5
  81.8 1.4 %multiply_reduce_fusion.1 = (f32[768]{0:T(1024)S(1)}, f32[400,768]{1,0:T(8,128)S(1)}) fusion(s32[512]{0:T(512)S(1)} %bitcast.36, f32[400,512]{1,0:T(8,128)S(1)} %multiply_add_fusion, f32[400,512]{1,0:T(8,128)S(1)} %copy-done.5), kind=kOutput, calls=%fused_computation.40 | convolution fusion | flops 1888648448 | bytes 2872320 | tf_op jit(solution)/shard_map/dot_general | solution.py:37
  83.2 0.6 sqrt_add_fusion.1
  83.8 0.0 copy-done.12
  83.8 1.2 %divide_subtract_fusion = f32[400,768]{1,0:T(8,128)} fusion(f32[400,768]{1,0:T(8,128)S(1)} %copy-done.12, f32[400,768]{1,0:T(8,128)S(1)} %get-tuple-element.35, f32[768]{0:T(1024)S(1)} %get-tuple-element.8), kind=kLoop, calls=%fused_computation.37 | loop fusion | flops 921600 | bytes 3689472 | tf_op jit(solution)/shard_map/sub | solution.py:42
  85.0 0.5 copy-done.1
  85.5 0.4 copy-done.3
  85.9 1.3 %divide_subtract_fusion.1 = f32[400,768]{1,0:T(8,128)} fusion(f32[400,768]{1,0:T(8,128)S(1)} %get-tuple-element.33, f32[768]{0:T(1024)S(1)} %get-tuple-element.10, f32[400,768]{1,0:T(8,128)S(1)} %copy-done.1, f32[768]{0:T(1024)S(1)} %sqrt_add_fusion.3, f32[400,768]{1,0:T(8,128)S(1)} %copy-done.3), kind=kLoop, calls=%fused_computation.39 | loop fusion | flops 1843200 | bytes 4921344 | tf_op jit(solution)/shard_map/sub | solution.py:42
  87.2 0.0 all-to-all-done
  87.2 0.1 reduce_sum.69
  87.3 0.8 copy-done.9
  88.1 0.1 copy-done.13
  88.2 0.8 divide_subtract_fusion.4
  (12 shorter events, 0.1 us)
Async XLA Ops:
  5.2 3.6 %copy-start = (f32[400,768]{1,0:T(8,128)S(1)}, f32[400,768]{1,0:T(8,128)}, u32[]{:S(2)}) copy-start(f32[400,768]{1,0:T(8,128)} %param.10) | copy-start | bytes 3686404
  13.8 2.5 %copy-start.15 = (f32[768]{0:T(1024)S(1)}, f32[768]{0:T(1024)}, u32[]{:S(2)}) copy-start(f32[768]{0:T(1024)} %param.13) | copy-start | bytes 9220
  13.8 2.5 %copy-start.10 = (f32[400,768]{1,0:T(8,128)S(1)}, f32[400,768]{1,0:T(8,128)}, u32[]{:S(2)}) copy-start(f32[400,768]{1,0:T(8,128)} %param.12) | copy-start | bytes 3686404
  16.5 40.8 %collective-permute-start = (f32[400,768]{1,0:T(8,128)S(1)}, f32[400,768]{1,0:T(8,128)S(1)}, u32[]{:S(2)}, u32[]{:S(2)}) collective-permute-start(f32[400,768]{1,0:T(8,128)S(1)} %divide_subtract_fusion.2), channel_id=1, source_target_pairs={{0,8},{8,16},{16,24},{24,32},{32,40},{40,48},{48,56},{56,64},{64,7... | collective-permute-start | bytes 3686408 | tf_op jit(solution)/shard_map/ppermute | solution.py:14
  20.1 1.4 %copy-start.14 = (f32[768]{0:T(1024)S(1)}, f32[768]{0:T(1024)}, u32[]{:S(2)}) copy-start(f32[768]{0:T(1024)} %param.11) | copy-start | bytes 9220
  20.1 1.4 %copy-start.8 = (f32[400,128]{1,0:T(8,128)S(1)}, f32[400,128]{1,0:T(8,128)}, u32[]{:S(2)}) copy-start(f32[400,128]{1,0:T(8,128)} %param.14) | copy-start | bytes 614404
  21.5 38.1 %copy-start.2 = (f32[400,768]{1,0:T(8,128)}, f32[400,768]{1,0:T(8,128)S(1)}, u32[]{:S(2)}) copy-start(f32[400,768]{1,0:T(8,128)S(1)} %get-tuple-element.30) | copy-start | bytes 3686404
  22.1 37.6 %copy-start.4 = (f32[400,512]{1,0:T(8,128)}, f32[400,512]{1,0:T(8,128)S(1)}, u32[]{:S(2)}) copy-start(f32[400,512]{1,0:T(8,128)S(1)} %convolution_bitcast_fusion) | copy-start | bytes 2457604
  57.3 2.3 %copy-start.11 = (f32[400,768]{1,0:T(8,128)}, f32[400,768]{1,0:T(8,128)S(1)}, u32[]{:S(2)}) copy-start(f32[400,768]{1,0:T(8,128)S(1)} %collective-permute-done) | copy-start | bytes 3686404
  61.1 2.1 %copy-start.6 = (f32[400,512]{1,0:T(8,128)}, f32[400,512]{1,0:T(8,128)S(1)}, u32[]{:S(2)}) copy-start(f32[400,512]{1,0:T(8,128)S(1)} %get-tuple-element.13) | copy-start | bytes 2457604
  66.6 20.6 %all-to-all-start = ((f32[8,400,128]{2,1,0:T(8,128)}), f32[8,400,128]{2,1,0:T(8,128)S(1)}, u32[]{:S(2)}, u32[]{:S(2)}) async-start(f32[8,400,128]{2,1,0:T(8,128)} %broadcast_in_dim.2), calls=%async_computation | async-start | bytes 3276800 | tf_op jit(solution)/shard_map/all_to_all | solution.py:19
  71.9 3.5 %copy-start.7 = (f32[400,512]{1,0:T(8,128)S(1)}, f32[400,512]{1,0:T(8,128)}, u32[]{:S(2)}) copy-start(f32[400,512]{1,0:T(8,128)} %copy-done.6) | copy-start | bytes 2457604
  71.9 9.4 %collective-permute-start.1 = (f32[768]{0:T(1024)S(1)}, f32[768]{0:T(1024)S(1)}, u32[]{:S(2)}, u32[]{:S(2)}) collective-permute-start(f32[768]{0:T(1024)S(1)} %get-tuple-element.15), channel_id=1, source_target_pairs={{0,8},{8,16},{16,24},{24,32},{32,40},{40,48},{48,56},{56,64},{64,7... | collective-permute-start | bytes 9224 | tf_op jit(solution)/shard_map/ppermute | solution.py:14
  76.9 4.9 %copy-start.5 = (f32[400,512]{1,0:T(8,128)S(1)}, f32[400,512]{1,0:T(8,128)}, u32[]{:S(2)}) copy-start(f32[400,512]{1,0:T(8,128)} %copy-done.4) | copy-start | bytes 2457604
  81.8 2.0 %copy-start.12 = (f32[400,768]{1,0:T(8,128)S(1)}, f32[400,768]{1,0:T(8,128)}, u32[]{:S(2)}) copy-start(f32[400,768]{1,0:T(8,128)} %copy-done.11) | copy-start | bytes 3686404
  83.8 1.7 %copy-start.1 = (f32[400,768]{1,0:T(8,128)S(1)}, f32[400,768]{1,0:T(8,128)}, u32[]{:S(2)}) copy-start(f32[400,768]{1,0:T(8,128)} %param.10) | copy-start | bytes 3686404
  83.8 2.1 %copy-start.3 = (f32[400,768]{1,0:T(8,128)S(1)}, f32[400,768]{1,0:T(8,128)}, u32[]{:S(2)}) copy-start(f32[400,768]{1,0:T(8,128)} %copy-done.2) | copy-start | bytes 3686404
  87.2 0.9 %copy-start.9 = (f32[400,128]{1,0:T(8,128)S(1)}, f32[400,128]{1,0:T(8,128)}, u32[]{:S(2)}) copy-start(f32[400,128]{1,0:T(8,128)} %param.14) | copy-start | bytes 614404
  87.2 1.0 %copy-start.13 = (f32[400,128]{1,0:T(8,128)S(1)}, f32[400,128]{1,0:T(8,128)}, u32[]{:S(2)}) copy-start(f32[400,128]{1,0:T(8,128)} %param.15) | copy-start | bytes 614404
where the time goes:
time: 89.6 us; the launch traced here: 89.1 us
  waiting for transfers between devices  36.6 us (41%)
  matrix products  29.5 us (33%)
  starting transfers between devices  9.62 us (11%)
  local copies, waits for them, and re-layouts  6.26 us (7%)
  other arithmetic  6.16 us (7%)
  between operations  0.99 us (1%)
    ppermute x2, waiting for transfers between devices, passed_along(): return lax.ppermute(value, axis, pairs)  36.6 us
    dot_general x6, matrix products, pick_columns(): return jnp.dot(matrix, selector, precision=HIGHEST)  10.6 us
    dot_general x6, matrix products, add_columns(): lax.dot_general(values, selector, (((1,), (1,)), ((), ())), precision=HIG...  8.69 us
    all_to_all x1, starting transfers between devices, sent_to_all(): lax.all_to_all(jnp.broadcast_to(x[None], (devices, *x.shape)), axis, 0, 0...  5.26 us
    ppermute x2, starting transfers between devices, passed_along(): return lax.ppermute(value, axis, pairs)  4.36 us
    dot_general x2, matrix products, bucket_terms(): lax.dot_general(queries, negative, (((0,), (0,)), ((), ())), precision=HI...  4.19 us
    dot_general x2, matrix products, bucket_terms(): lax.dot_general(negative, neg_coef, (((1,), (1,)), ((), ())), precision=H...  3.01 us
    dot_general x2, matrix products, bucket_terms(): grad_negative = jnp.dot(queries, neg_coef, precision=HIGHEST)  2.99 us
  transfers between devices with their start and end apart: 3, of which 2 were waited for; matrix products, arithmetic and copies ran while one was open for 16% of the time, Pallas kernels for 0%

commit v1 on v0

v1 whole, which is shorter than its diff:
```python
import functools

import jax
import jax.numpy as jnp
from jax import lax
from jax.experimental import pallas as pl
from jax.experimental.pallas import tpu as pltpu
from jax.sharding import PartitionSpec as P

LR = 0.1
EPS = 1e-06
F32 = jnp.float32
BF16 = jnp.bfloat16
VMEM_LIMIT = 32 * 1024 * 1024
TILE = 256
NEAR = 512


def split(x):
    hi = x.astype(BF16)
    lo = (x - hi.astype(F32)).astype(BF16)
    return hi, lo


def dot(a, b):
    return jnp.dot(a, b, preferred_element_type=F32)


def dot_nt(a, b):
    return lax.dot_general(a, b, (((1,), (1,)), ((), ())), preferred_element_type=F32)


def column(row):
    n = row.shape[1]
    return jnp.transpose(jnp.broadcast_to(row, (8, n)))[:, 0:1]


def hot_down(row, length):
    n = row.shape[1]
    spots = lax.broadcasted_iota(jnp.int32, (length, n), 0)
    return jnp.where(spots == row, 1.0, 0.0).astype(BF16)


def hot_along(col, length, start=0):
    n = col.shape[0]
    spots = lax.broadcasted_iota(jnp.int32, (n, length), 1) + start
    return jnp.where(spots == col, 1.0, 0.0).astype(BF16)


def picked(matrix, hot):
    hi, lo = split(matrix)
    return dot(hi, hot) + dot(lo, hot)


def weights(q_t, t, target_col, negative_col, start, negatives):
    (qa, qb), (ta, tb) = q_t, split(t)
    score = dot(qa, ta) + dot(qa, tb) + dot(qb, ta)
    spots = lax.broadcasted_iota(jnp.int32, score.shape, 1) + start
    count = jnp.sum(jnp.where(spots == negative_col, 1.0 / negatives, 0.0), axis=0, keepdims=True)
    level = jax.nn.sigmoid(score)
    return level * count + jnp.where(spots == target_col, level - 1.0, 0.0)


def stepped(matrix, state, grad):
    fresh = state + jnp.sum(grad * grad, axis=0, keepdims=True) * (1.0 / grad.shape[0])
    return matrix - grad * (LR / (jnp.sqrt(fresh) + EPS)), fresh


def started(copies):
    out = [pltpu.make_async_copy(src, dst, sem) for src, dst, sem in copies]
    for c in out:
        c.start()
    return out


def near_body(bucket, s_in, t_in, tst_in, r_in, sid_in, tid_in, rid_in, nid_in,
              near_ref, src_ref, rel_ref, qa_ref, qb_ref, qta_ref, qtb_ref, wa_ref, wb_ref,
              s_ref, t_ref, tst_ref, r_ref, sid_ref, tid_ref, rid_ref, nid_ref, sems):
    d, rows = t_ref.shape
    c_sid, c_rid, c_r, c_s, c_tid, c_nid, c_tst, c_t = started([
        (sid_in, sid_ref, sems.at[0]), (rid_in, rid_ref, sems.at[1]), (r_in, r_ref, sems.at[2]),
        (s_in, s_ref, sems.at[3]), (tid_in, tid_ref, sems.at[4]), (nid_in, nid_ref, sems.at[5]),
        (tst_in, tst_ref, sems.at[6]), (t_in.at[:, 0:NEAR], t_ref.at[:, 0:NEAR], sems.at[7])])
    c_sid.wait()
    c_rid.wait()
    hot_s = hot_down(sid_ref[bucket:bucket + 1, :], rows)
    hot_r = hot_down(rid_ref[bucket:bucket + 1, :], r_ref.shape[1])
    c_r.wait()
    rel = picked(r_ref[...], hot_r)
    c_s.wait()
    src = picked(s_ref[...], hot_s)
    src_ref[...] = src
    rel_ref[...] = rel
    q = src * rel
    qa, qb = split(q)
    qa_ref[...] = qa
    qb_ref[...] = qb
    q_t = split(jnp.transpose(q))
    qta_ref[...], qtb_ref[...] = q_t
    c_tid.wait()
    c_nid.wait()
    target_col = column(tid_ref[bucket:bucket + 1, :])
    negative_col = column(nid_ref[bucket:bucket + 1, :])
    c_tst.wait()
    c_t.wait()
    for start in range(0, NEAR, TILE):
        cols = slice(start, start + TILE)
        t = t_ref[:, cols]
        wa, wb = split(weights(q_t, t, target_col, negative_col, start, nid_ref.shape[1]))
        wa_ref[:, cols] = wa
        wb_ref[:, cols] = wb
        grad = dot(qa, wa) + dot(qb, wa) + dot(qa, wb)
        t_new, fresh = stepped(t, tst_ref[cols][None], grad)
        near_ref[0:d, cols] = t_new
        near_ref[d:d + 8, cols] = jnp.broadcast_to(fresh, (8, TILE))


def far_body(bucket, t_in, tst_in, tid_in, nid_in, qa_ref, qb_ref, qta_ref, qtb_ref,
             far_ref, wa_ref, wb_ref,
             t_ref, tst_ref, tid_ref, nid_ref, sems):
    d = t_ref.shape[0]
    copies = started([
        (tid_in, tid_ref, sems.at[0]), (nid_in, nid_ref, sems.at[1]), (tst_in, tst_ref, sems.at[2]),
        (t_in.at[:, NEAR:], t_ref, sems.at[3])])
    for c in copies:
        c.wait()
    q_t = (qta_ref[...], qtb_ref[...])
    qa, qb = qa_ref[...], qb_ref[...]
    target_col = column(tid_ref[bucket:bucket + 1, :])
    negative_col = column(nid_ref[bucket:bucket + 1, :])
    t = t_ref[...]
    wa, wb = split(weights(q_t, t, target_col, negative_col, NEAR, nid_ref.shape[1]))
    wa_ref[...] = wa
    wb_ref[...] = wb
    grad = dot(qa, wa) + dot(qb, wa) + dot(qa, wb)
    t_new, fresh = stepped(t, tst_ref[NEAR:][None], grad)
    far_ref[0:d, :] = t_new
    far_ref[d:d + 8, :] = jnp.broadcast_to(fresh, (8, t.shape[1]))


def source_body(bucket, s_in, sst_in, t_in, r_in, sid_in, rid_in,
                src_ref, rel_ref, wna_ref, wnb_ref, wfa_ref, wfb_ref,
                snew_out, sst_out, rel2_out, qa_out, qb_out, rgrad_ref, src2_ref, qta_ref, qtb_ref,
                s_ref, sst_ref, t_ref, r_ref, sid_ref, rid_ref,
                snew_ref, sstnew_ref, rel2_ref, qa_ref, qb_ref, sems):
    d, rows = s_ref.shape
    copies = started([
        (t_in, t_ref, sems.at[0]), (sid_in, sid_ref, sems.at[1]), (rid_in, rid_ref, sems.at[2]),
        (r_in, r_ref, sems.at[3]), (s_in, s_ref, sems.at[4]), (sst_in, sst_ref, sems.at[5])])
    copies[0].wait()
    ta, tb = split(t_ref[:, 0:NEAR])
    gq = dot_nt(ta, wna_ref[...]) + dot_nt(tb, wna_ref[...]) + dot_nt(ta, wnb_ref[...])
    ta, tb = split(t_ref[:, NEAR:])
    gq += dot_nt(ta, wfa_ref[...]) + dot_nt(tb, wfa_ref[...]) + dot_nt(ta, wfb_ref[...])
    for c in copies[1:]:
        c.wait()
    rid_col = column(rid_ref[bucket:bucket + 1, :])
    sid_col = column(sid_ref[bucket:bucket + 1, :])
    rgrad_ref[...] = picked(gq * src_ref[...], hot_along(rid_col, r_ref.shape[1]))
    grad = picked(gq * rel_ref[...], hot_along(sid_col, rows))
    s_new, fresh = stepped(s_ref[...], sst_ref[...][None], grad)
    snew_ref[...] = s_new
    sstnew_ref[...] = fresh[0]
    outs = started([(snew_ref, snew_out, sems.at[6]), (sstnew_ref, sst_out, sems.at[7])])
    after = bucket + 1
    src = picked(s_new, hot_down(sid_ref[after:after + 1, :], rows))
    rel = picked(r_ref[...], hot_down(rid_ref[after:after + 1, :], r_ref.shape[1]))
    src2_ref[...] = src
    rel2_ref[...] = rel
    q = src * rel
    qa_ref[...], qb_ref[...] = split(q)
    outs += started([(rel2_ref, rel2_out, sems.at[8]), (qa_ref, qa_out, sems.at[9]), (qb_ref, qb_out, sems.at[10])])
    qta_ref[...], qtb_ref[...] = split(jnp.transpose(q))
    for c in outs:
        c.wait()


def query_body(bucket, direct_ref, relayed_ref, near_ref, src_ref, qta_ref, qtb_ref, rgrad_ref,
               tid_ref, rid_ref, nid_ref,
               gq_out, wa_out, wb_out, t_out, sum_ref,
               gq_ref, wa_ref, wb_ref, t_ref, sems):
    d = src_ref.shape[0]
    rows = t_ref.shape[1]
    q_t = (qta_ref[...], qtb_ref[...])
    target_col = column(tid_ref[bucket:bucket + 1, :])
    negative_col = column(nid_ref[bucket:bucket + 1, :])
    gq = jnp.zeros(src_ref.shape, F32)
    outs = []
    for start in range(0, rows, TILE):
        cols = slice(start, start + TILE)
        if start < NEAR:
            t_all = near_ref[:, cols]
        else:
            away = slice(start - NEAR, start - NEAR + TILE)
            t_all = direct_ref[:, away] + relayed_ref[:, away]
        t_ref[:, cols] = t_all
        t = t_all[0:d]
        wa, wb = split(weights(q_t, t, target_col, negative_col, start, nid_ref.shape[1]))
        wa_ref[:, cols] = wa
        wb_ref[:, cols] = wb
        ta, tb = split(t)
        gq += dot_nt(ta, wa) + dot_nt(tb, wa) + dot_nt(ta, wb)
    gq_ref[...] = gq
    outs = started([(gq_ref, gq_out, sems.at[0]), (wa_ref, wa_out, sems.at[1]), (wb_ref, wb_out, sems.at[2]),
                    (t_ref, t_out, sems.at[3])])
    rid_col = column(rid_ref[bucket:bucket + 1, :])
    total = rgrad_ref[...] + picked(gq * src_ref[...], hot_along(rid_col, rgrad_ref.shape[1]))
    sum_ref[0:d, :] = total
    if sum_ref.shape[0] > d:
        sum_ref[d:, :] = jnp.zeros((sum_ref.shape[0] - d, total.shape[1]), F32)
    for c in outs:
        c.wait()


def target_body(t_in, qa_in, qb_in, wa_in, wb_in, tnew_out, tst_out,
                t_ref, qa_ref, qb_ref, wa_ref, wb_ref, tnew_ref, tst_ref, sems):
    d, rows = tnew_ref.shape
    copies = started([
        (qa_in, qa_ref, sems.at[0]), (qb_in, qb_ref, sems.at[1]), (wa_in, wa_ref, sems.at[2]),
        (wb_in, wb_ref, sems.at[3]), (t_in, t_ref, sems.at[4])])
    for c in copies:
        c.wait()
    qa, qb = qa_ref[...], qb_ref[...]
    outs = []
    for i, start in enumerate(range(0, rows, TILE)):
        cols = slice(start, start + TILE)
        wa, wb = wa_ref[:, cols], wb_ref[:, cols]
        grad = dot(qa, wa) + dot(qb, wa) + dot(qa, wb)
        t_new, fresh = stepped(t_ref[0:d, cols], t_ref[d:d + 1, cols], grad)
        tnew_ref[:, cols] = t_new
        tst_ref[cols] = fresh[0]
        outs += started([(tnew_ref.at[:, cols], tnew_out.at[:, cols], sems.at[5 + i])])
    outs += started([(tst_ref, tst_out, sems.at[4])])
    for c in outs:
        c.wait()


def last_source_body(bucket, s_in, sst_in, gq_in, rel_in, sid_in, snew_out, sst_out,
                     s_ref, sst_ref, gq_ref, rel_ref, sid_ref, snew_ref, sstnew_ref, sems):
    d, rows = s_ref.shape
    copies = started([
        (gq_in, gq_ref, sems.at[0]), (rel_in, rel_ref, sems.at[1]), (sid_in, sid_ref, sems.at[2]),
        (s_in, s_ref, sems.at[3]), (sst_in, sst_ref, sems.at[4])])
    for c in copies:
        c.wait()
    sid_col = column(sid_ref[bucket:bucket + 1, :])
    ga, gb = split(gq_ref[...] * rel_ref[...])
    outs = []
    for i, start in enumerate(range(0, rows, TILE)):
        cols = slice(start, start + TILE)
        hot = hot_along(sid_col, TILE, start)
        s_new, fresh = stepped(s_ref[:, cols], sst_ref[cols][None], dot(ga, hot) + dot(gb, hot))
        snew_ref[:, cols] = s_new
        sstnew_ref[cols] = fresh[0]
        outs += started([(snew_ref.at[:, cols], snew_out.at[:, cols], sems.at[5 + i])])
    outs += started([(sstnew_ref, sst_out, sems.at[4])])
    for c in outs:
        c.wait()


def total_body(parts_ref, out_ref):
    own = parts_ref[0]
    for i in range(1, parts_ref.shape[0]):
        own += parts_ref[i]
    for i in range(out_ref.shape[0]):
        out_ref[i] = own


HBM, VM = pltpu.HBM, pltpu.VMEM


def call(body, ins, outs, scratch=(), flops=0):
    moved = sum(a.size * a.dtype.itemsize for _, a in (*ins, *outs))
    return pl.pallas_call(
        body,
        out_shape=[m(a.shape, a.dtype) for m, a in outs],
        in_specs=[pl.BlockSpec(memory_space=m) for m, _ in ins],
        out_specs=[pl.BlockSpec(memory_space=m) for m, _ in outs],
        scratch_shapes=list(scratch),
        compiler_params=pltpu.CompilerParams(vmem_limit_bytes=VMEM_LIMIT),
        cost_estimate=pl.CostEstimate(flops=flops, bytes_accessed=moved, transcendentals=0),
    )(*[pltpu.with_memory_space_constraint(a, m) for m, a in ins])


def of(spec, *arrays):
    return [(spec, a) for a in arrays]


def room(*arrays):
    return [pltpu.VMEM(a.shape, a.dtype) for a in arrays]


def per_device(s, sst, t, tst, r, rst, sid, tid, rid, nid):
    d, rows = s.shape
    edges = sid.shape[1]
    rels = r.shape[1]
    away = rows - NEAR
    shape = jax.ShapeDtypeStruct
    sems = pltpu.SemaphoreType.DMA((12,))
    wide = shape((d, edges), F32)
    thin = shape((d, edges), BF16)
    thin_t = shape((edges, d), BF16)
    full = shape((d, rows), F32)
    held = shape((d + 8, rows), F32)
    line = shape((rows,), F32)
    half = shape((edges, rows), BF16)
    near_w = shape((edges, NEAR), BF16)
    far_w = shape((edges, away), BF16)
    unit = 2 * d * rows * edges

    near, src0, rel0, qa0, qb0, qta0, qtb0, wna, wnb = call(
        functools.partial(near_body, 0),
        of(HBM, s, t, tst, r, sid, tid, rid, nid),
        of(VM, shape((d + 8, NEAR), F32), wide, wide, thin, thin, thin_t, thin_t, near_w, near_w),
        [*room(s, t, tst, r, sid, tid, rid, nid), sems], flops=7 * unit)
    far, wfa, wfb = call(
        functools.partial(far_body, 0),
        of(HBM, t, tst, tid, nid) + of(VM, qa0, qb0, qta0, qtb0),
        of(VM, shape((d + 8, away), F32), far_w, far_w),
        [pltpu.VMEM((d, away), F32), *room(tst, tid, nid), sems], flops=2 * unit)

    count = lax.axis_size("blk")
    run = 16
    ring = [(i, (i + 1) % count) for i in range(count)]
    turns = [p for p in ring if p[1] % run == 0]
    first_leg = [(a, (b + run - 2) % count) for a, b in turns]
    second_leg = [((b + run - 2) % count, b) for a, b in turns]
    near = lax.ppermute(near, "blk", ring)
    leg = lax.ppermute(far, "blk", first_leg)
    direct = lax.ppermute(far, "blk", [p for p in ring if p not in turns])
    s1, sst1, rel1, qa1, qb1, rgrad0, src1, qta1, qtb1 = call(
        functools.partial(source_body, 0),
        of(HBM, s, sst, t, r, sid, rid) + of(VM, src0, rel0, wna, wnb, wfa, wfb),
        of(HBM, full, line, wide, thin, thin) + of(VM, shape((d, rels), F32), wide, thin_t, thin_t),
        [*room(s, sst, t, r, sid, rid, full, line, wide, thin, thin), sems], flops=9 * unit)
    relayed = lax.ppermute(leg, "blk", second_leg)

    group = lax.axis_size("rel")
    piece = -(-d // (8 * group)) * 8
    gq1, wa1, wb1, t1, total = call(
        functools.partial(query_body, 1),
        of(VM, direct, relayed, near, src1, qta1, qtb1, rgrad0, tid, rid, nid),
        of(HBM, wide, half, half, held) + of(VM, shape((piece * group, rels), F32)),
        [*room(wide, half, half, held), sems], flops=7 * unit)
    parts = lax.all_to_all(total.reshape(group, piece, rels), "rel", 0, 0, tiled=True)
    t2, tst2 = call(
        target_body,
        of(HBM, t1, qa1, qb1, wa1, wb1),
        of(HBM, full, line),
        [*room(held, thin, thin, half, half, full, line), sems], flops=3 * unit)
    parts, t2 = lax.optimization_barrier((parts, t2))
    (own,) = call(total_body, of(VM, parts), of(VM, shape(parts.shape, F32)))
    every = lax.all_to_all(own, "rel", 0, 0, tiled=True)
    s2, sst2 = call(
        functools.partial(last_source_body, 1),
        of(HBM, s1, sst1, gq1, rel1, sid),
        of(HBM, full, line),
        [*room(s1, sst1, gq1, rel1, sid, full, line), sems], flops=2 * unit)
    summed = every.reshape(piece * group, rels)[:d]
    rst1 = rst + summed * summed
    r1 = r - LR * summed / (jnp.sqrt(rst1) + EPS)
    return s2, sst2, t2, tst2, r1, rst1


def solution(mesh):
    both = ("blk", "rel")
    placed = (
        P(None, both), P(both), P(None, both), P(both), P(None, "blk"), P(None, "blk"),
        P(None, both), P(None, both), P(None, both), P(None, both),
    )
    return jax.shard_map(
        per_device,
        mesh=mesh,
        in_specs=placed,
        out_specs=placed[:6],
        check_vma=False,
    )
```

time: 89.6 us -> 72.3 us (0.81)
  Pallas kernels: 0 us -> 31 us
  matrix products: 29.5 us -> 0 us
  waiting for transfers between devices: 36.6 us -> 17.8 us
  starting transfers between devices: 9.62 us -> 21.4 us
  local copies, waits for them, and re-layouts: 6.26 us -> 0.03 us
  other arithmetic: 6.16 us -> 0.84 us
    pallas_call x0 -> x7, Pallas kernels: none -> 31 us  [call(): pl.pallas_call(body, out_shape=[m(a.shape, a.dtype) for m, a in outs], in...]
    dot_general x18 -> x0, matrix products: 29.5 us -> none  [the longest x6 10.6 us: pick_columns(): return jnp.dot(matrix, selector, precision=HIGHEST)]
    ppermute x2 -> x4, waiting for transfers between devices: 36.6 us -> 15.5 us  [the longest x1 15.5 us: per_device(): near = lax.ppermute(near, 'blk', ring)]
    all_to_all x1 -> x2, starting transfers between devices: 5.26 us -> 13.9 us  [the longest x1 8.78 us: per_device(): lax.all_to_all(total.reshape(group, piece, rels), 'rel', 0, 0, tiled=True)]
    ppermute x2 -> x4, starting transfers between devices: 4.36 us -> 7.51 us  [the longest x1 3.61 us: per_device(): direct = lax.ppermute(far, 'blk', [p for p in ring if p not in turns])]
    slice x4 -> x0, local copies, waits for them, and re-layouts: 3.07 us -> none  [the longest x1 0.77 us: per_device(): source_ids[bucket]]
    sub x4 -> x1, other arithmetic: 3.49 us -> 0.84 us  [per_device(): r1 = r - LR * summed / (jnp.sqrt(rst1) + EPS)]
    all_to_all x1 -> x2, waiting for transfers between devices: 0.01 us -> 2.33 us  [the longest x1 1.27 us: per_device(): every = lax.all_to_all(own, 'rel', 0, 0, tiled=True)]
  transfers between devices with their start and end apart: 3 -> 6, of which waited for: 2 -> 3; matrix products, arithmetic and copies ran while one was open for 16% -> 0% of each run, Pallas kernels for 0% -> 25%
where the time goes in v1:
time: 72.3 us; the launch traced here: 71.8 us
  Pallas kernels  31 us (43%)
  starting transfers between devices  21.4 us (30%)
  waiting for transfers between devices  17.8 us (25%)
  other arithmetic  0.84 us (1%)
  between operations  0.77 us (1%)
    pallas_call x7, Pallas kernels, call(): pl.pallas_call(body, out_shape=[m(a.shape, a.dtype) for m, a in outs], in...  31 us
    ppermute x1, waiting for transfers between devices, per_device(): near = lax.ppermute(near, 'blk', ring)  15.5 us
    all_to_all x1, starting transfers between devices, per_device(): lax.all_to_all(total.reshape(group, piece, rels), 'rel', 0, 0, tiled=True)  8.78 us
    all_to_all x1, starting transfers between devices, per_device(): every = lax.all_to_all(own, 'rel', 0, 0, tiled=True)  5.07 us
    ppermute x1, starting transfers between devices, per_device(): direct = lax.ppermute(far, 'blk', [p for p in ring if p not in turns])  3.61 us
    ppermute x1, starting transfers between devices, per_device(): near = lax.ppermute(near, 'blk', ring)  1.92 us
  transfers between devices with their start and end apart: 6, of which 3 were waited for; matrix products, arithmetic and copies ran while one was open for 0% of the time, Pallas kernels for 25%

profile of v1, /device:TPU:2, one launch (start us, length us, event | category | flops | bytes accessed | tf_op | source)
XLA Modules:
  0.0 71.8 jit_solution(540099262305214834)
XLA Ops:
  0.6 6.3 %shard_map.145 = (f32[408,512]{1,0:T(8,128)S(1)}, f32[400,512]{1,0:T(8,128)S(1)}, f32[400,512]{1,0:T(8,128)S(1)}, bf16[400,512]{1,0:T(8,128)(2,1)S(1)}, bf16[400...) custom-call(f32[400,768]{1,0:T(8,128)} %s_in.3, ...), custom_call_target="tpu_custom_call" | custom-call | flops 2202009600 | bytes 7842816 | tf_op jit(solution)/shard_map/pallas_call | solution.py:274
  6.9 1.9 %collective-permute-start.3 = (f32[408,512]{1,0:T(8,128)S(1)}, f32[408,512]{1,0:T(8,128)S(1)}, u32[]{:S(2)}, u32[]{:S(2)}) collective-permute-start(f32[408,512]{1,0:T(8,128)S(1)} %get-tuple-element.51), channel_id=1, source_target_pairs={{0,8},{8,16},{16,24},{24,32},{32,40},{40,48},{48,56},{56,64},{64,7... | collective-permute-start | bytes 2506760 | tf_op jit(solution)/shard_map/ppermute | solution.py:328
  8.8 2.9 %shard_map.146 = (f32[408,256]{1,0:T(8,128)S(1)}, bf16[512,256]{1,0:T(8,128)(2,1)S(1)}, bf16[512,256]{1,0:T(8,128)(2,1)S(1)}) custom-call(f32[400,768]{1,0:T(8,128)} %t_in.5, f32[768]{0:T(1024)} %tst_in.3, s32[2,512]{1,0:T(2,128)} %tid_ref.1, s32[2,512]{1,0:T(2,128)} %nid_ref.1, bf16[400,512]{1,0:T(8,128)(2,1)S(1)} %get-tuple-element.42.qa_ref, ...), custom_call_target="tpu_custom_call" | custom-call | flops 629145600 | bytes 3820544 | tf_op jit(solution)/shard_map/pallas_call | solution.py:274
  11.7 0.7 collective-permute-start.1
  12.4 3.6 %collective-permute-start = (f32[408,256]{1,0:T(8,128)S(1)}, f32[408,256]{1,0:T(8,128)S(1)}, u32[]{:S(2)}, u32[]{:S(2)}) collective-permute-start(f32[408,256]{1,0:T(8,128)S(1)} %get-tuple-element.50), channel_id=1, source_target_pairs={{0,8},{8,16},{16,24},{24,32},{32,40},{40,48},{48,56},{56,64},{64,7... | collective-permute-start | bytes 1253384 | tf_op jit(solution)/shard_map/ppermute | solution.py:330
  16.0 0.0 collective-permute-done.1
  16.0 1.3 %collective-permute-start.2 = (f32[408,256]{1,0:T(8,128)S(1)}, f32[408,256]{1,0:T(8,128)S(1)}, u32[]{:S(2)}, u32[]{:S(2)}) collective-permute-start(f32[408,256]{1,0:T(8,128)S(1)} %collective-permute-done.1), channel_id=1, source_target_pairs={{240,128},{368,256},{496,384},{112,0},{241,129},{369,257},{497,385... | collective-permute-start | bytes 1253384 | tf_op jit(solution)/shard_map/ppermute | solution.py:336
  17.3 0.0 copy-start
  17.3 0.0 copy-start.1
  17.3 0.0 copy-start.2
  17.4 6.5 %shard_map.147 = (f32[400,768]{1,0:T(8,128)}, f32[768]{0:T(1024)}, f32[400,512]{1,0:T(8,128)}, bf16[400,512]{1,0:T(8,128)(2,1)}, bf16[400,512]{1,0:T(8,128)(2,1)...) custom-call(f32[400,768]{1,0:T(8,128)} %s_in.3, ...), custom_call_target="tpu_custom_call" | custom-call | flops 2831155200 | bytes 10598400 | tf_op jit(solution)/shard_map/pallas_call | solution.py:274
  23.8 0.0 collective-permute-done.direct_ref
  23.8 15.5 %collective-permute-done.3.near_ref = f32[408,512]{1,0:T(8,128)S(1)} collective-permute-done((f32[408,512]{1,0:T(8,128)S(1)}, f32[408,512]{1,0:T(8,128)S(1)}, u32[]{:S(2)}, u32[]{:S(2)}) %collective-permute-start.3) | collective-permute-done | bytes 835616 | tf_op jit(solution)/shard_map/ppermute | solution.py:328
  39.3 0.0 collective-permute-done.2.relayed_ref
  39.3 0.0 copy-done
  39.3 0.0 copy-done.1
  39.3 0.0 copy-done.2
  39.4 6.4 %shard_map.148 = (f32[400,512]{1,0:T(8,128)}, bf16[512,768]{1,0:T(8,128)(2,1)}, bf16[512,768]{1,0:T(8,128)(2,1)}, f32[408,768]{1,0:T(8,128)}, f32[448,128]{1,0:T(8,128)}) custom-call(f32[408,256]{1,0:T(8,128)S(1)} %collective-permute-done.direct_ref, f32[408,256]{1,0:T(8,128)S(1)} %collective-permute-done.2.relayed_ref, ...), custom_call_target="tpu_custom_call" | custom-call | flops 2202009600 | bytes 7401472 | tf_op jit(solution)/shard_map/pallas_call | solution.py:274
  45.7 8.8 %all-to-all-start = ((f32[8,56,128]{2,1,0:T(8,128)}), f32[8,56,128]{2,1,0:T(8,128)S(1)}, u32[]{:S(2)}, u32[]{:S(2)}) async-start(f32[8,56,128]{2,1,0:T(8,128)} %bitcast), calls=%async_computation | async-start | bytes 458752 | tf_op jit(solution)/shard_map/all_to_all | solution.py:345
  54.5 4.3 %shard_map.150 = (f32[400,768]{1,0:T(8,128)}, f32[768]{0:T(1024)}) custom-call(f32[408,768]{1,0:T(8,128)} %get-tuple-element.61.t_in, bf16[400,512]{1,0:T(8,128)(2,1)} %get-tuple-element.62.qa_in, bf16[400,512]{1,0:T(8,128)(2,1)} %get-tuple-element.63.qb_in, bf16[512,768]{1,0:T(8,128)(2,1)} %get-tuple-element.64.wa_in, bf16[512,768]{1,0:T(8,128)(2,1)} %get-tuple-element.65.wb_in), custom_call_target="tpu_custom_call" | custom-call | flops 943718400 | bytes 4877312 | tf_op jit(solution)/shard_map/pallas_call | solution.py:274
  58.8 1.1 %all-to-all-done.parts_ref = f32[8,56,128]{2,1,0:T(8,128)S(1)} async-done(((f32[8,56,128]{2,1,0:T(8,128)}), f32[8,56,128]{2,1,0:T(8,128)S(1)}, u32[]{:S(2)}, u32[]{:S(2)}) %all-to-all-start) | async-done | bytes 229408 | tf_op jit(solution)/shard_map/all_to_all | solution.py:345
  59.9 0.7 shard_map.151
  60.5 5.1 %all-to-all-start.1 = ((f32[8,56,128]{2,1,0:T(8,128)}), f32[8,56,128]{2,1,0:T(8,128)S(1)}, u32[]{:S(2)}, u32[]{:S(2)}) async-start(f32[8,56,128]{2,1,0:T(8,128)} %shard_map.151), calls=%async_computation.1 | async-start | bytes 458752 | tf_op jit(solution)/shard_map/all_to_all | solution.py:353
  65.6 0.0 copy-start.3
  65.6 0.0 copy-start.4
  65.6 4.1 %shard_map.149 = (f32[400,768]{1,0:T(8,128)}, f32[768]{0:T(1024)}) custom-call(f32[400,768]{1,0:T(8,128)} %get-tuple-element.48.s_in, f32[768]{0:T(1024)} %get-tuple-element.49.sst_in, f32[400,512]{1,0:T(8,128)} %get-tuple-element.56.gq_in, f32[400,512]{1,0:T(8,128)} %get-tuple-element.57.rel_in, s32[2,512]{1,0:T(2,128)} %sid_in.5), custom_call_target="tpu_custom_call" | custom-call | flops 629145600 | bytes 4106240 | tf_op jit(solution)/shard_map/pallas_call | solution.py:274
  69.7 1.3 %all-to-all-done.1 = f32[8,56,128]{2,1,0:T(8,128)S(1)} async-done(((f32[8,56,128]{2,1,0:T(8,128)}), f32[8,56,128]{2,1,0:T(8,128)S(1)}, u32[]{:S(2)}, u32[]{:S(2)}) %all-to-all-start.1) | async-done | bytes 229408 | tf_op jit(solution)/shard_map/all_to_all | solution.py:353
  71.0 0.0 copy-done.3
  71.0 0.0 copy-done.4
  71.0 0.8 %divide_subtract_fusion = (f32[400,128]{1,0:T(8,128)}, f32[400,128]{1,0:T(8,128)}) fusion(f32[400,128]{1,0:T(8,128)S(1)} %copy-done.3, f32[448,128]{1,0:T(8,128)S(1)} %bitcast.2, f32[400,128]{1,0:T(8,128)S(1)} %copy-done.4), kind=kLoop, calls=%fused_computation | loop fusion | flops 307200 | bytes 1024000 | tf_op jit(solution)/shard_map/sub | solution.py:361
Async XLA Ops:
  6.9 32.4 %collective-permute-start.3 = (f32[408,512]{1,0:T(8,128)S(1)}, f32[408,512]{1,0:T(8,128)S(1)}, u32[]{:S(2)}, u32[]{:S(2)}) collective-permute-start(f32[408,512]{1,0:T(8,128)S(1)} %get-tuple-element.51), channel_id=1, source_target_pairs={{0,8},{8,16},{16,24},{24,32},{32,40},{40,48},{48,56},{56,64},{64,7... | collective-permute-start | bytes 2506760 | tf_op jit(solution)/shard_map/ppermute | solution.py:328
  11.7 4.3 %collective-permute-start.1 = (f32[408,256]{1,0:T(8,128)S(1)}, f32[408,256]{1,0:T(8,128)S(1)}, u32[]{:S(2)}, u32[]{:S(2)}) collective-permute-start(f32[408,256]{1,0:T(8,128)S(1)} %get-tuple-element.50), channel_id=1, source_target_pairs={{120,240},{248,368},{376,496},{504,112},{121,241},{249,369},{377,4... | collective-permute-start | bytes 1253384 | tf_op jit(solution)/shard_map/ppermute | solution.py:329
  12.4 11.4 %collective-permute-start = (f32[408,256]{1,0:T(8,128)S(1)}, f32[408,256]{1,0:T(8,128)S(1)}, u32[]{:S(2)}, u32[]{:S(2)}) collective-permute-start(f32[408,256]{1,0:T(8,128)S(1)} %get-tuple-element.50), channel_id=1, source_target_pairs={{0,8},{8,16},{16,24},{24,32},{32,40},{40,48},{48,56},{56,64},{64,7... | collective-permute-start | bytes 1253384 | tf_op jit(solution)/shard_map/ppermute | solution.py:330
  16.0 23.3 %collective-permute-start.2 = (f32[408,256]{1,0:T(8,128)S(1)}, f32[408,256]{1,0:T(8,128)S(1)}, u32[]{:S(2)}, u32[]{:S(2)}) collective-permute-start(f32[408,256]{1,0:T(8,128)S(1)} %collective-permute-done.1), channel_id=1, source_target_pairs={{240,128},{368,256},{496,384},{112,0},{241,129},{369,257},{497,385... | collective-permute-start | bytes 1253384 | tf_op jit(solution)/shard_map/ppermute | solution.py:336
  17.3 22.0 %copy-start = (s32[2,512]{1,0:T(2,128)S(1)}, s32[2,512]{1,0:T(2,128)}, u32[]{:S(2)}) copy-start(s32[2,512]{1,0:T(2,128)} %tid_ref.1) | copy-start | bytes 12292
  17.3 22.0 %copy-start.1 = (s32[2,512]{1,0:T(2,128)S(1)}, s32[2,512]{1,0:T(2,128)}, u32[]{:S(2)}) copy-start(s32[2,512]{1,0:T(2,128)} %nid_ref.1) | copy-start | bytes 12292
  17.3 22.0 %copy-start.2 = (s32[2,512]{1,0:T(2,128)S(1)}, s32[2,512]{1,0:T(2,128)}, u32[]{:S(2)}) copy-start(s32[2,512]{1,0:T(2,128)} %rid_ref.1) | copy-start | bytes 12292
  45.7 14.1 %all-to-all-start = ((f32[8,56,128]{2,1,0:T(8,128)}), f32[8,56,128]{2,1,0:T(8,128)S(1)}, u32[]{:S(2)}, u32[]{:S(2)}) async-start(f32[8,56,128]{2,1,0:T(8,128)} %bitcast), calls=%async_computation | async-start | bytes 458752 | tf_op jit(solution)/shard_map/all_to_all | solution.py:345
  60.5 10.4 %all-to-all-start.1 = ((f32[8,56,128]{2,1,0:T(8,128)}), f32[8,56,128]{2,1,0:T(8,128)S(1)}, u32[]{:S(2)}, u32[]{:S(2)}) async-start(f32[8,56,128]{2,1,0:T(8,128)} %shard_map.151), calls=%async_computation.1 | async-start | bytes 458752 | tf_op jit(solution)/shard_map/all_to_all | solution.py:353
  65.6 5.4 %copy-start.3 = (f32[400,128]{1,0:T(8,128)S(1)}, f32[400,128]{1,0:T(8,128)}, u32[]{:S(2)}) copy-start(f32[400,128]{1,0:T(8,128)} %r_in.3) | copy-start | bytes 614404
  65.6 5.4 %copy-start.4 = (f32[400,128]{1,0:T(8,128)S(1)}, f32[400,128]{1,0:T(8,128)}, u32[]{:S(2)}) copy-start(f32[400,128]{1,0:T(8,128)} %param.15) | copy-start | bytes 614404

commit v2 on v1

v2 whole, which is shorter than its diff:
```python
import functools

import jax
import jax.numpy as jnp
from jax import lax
from jax.experimental import pallas as pl
from jax.experimental.pallas import tpu as pltpu
from jax.sharding import PartitionSpec as P

LR = 0.1
EPS = 1e-06
F32 = jnp.float32
BF16 = jnp.bfloat16
VMEM_LIMIT = 32 * 1024 * 1024
TILE = 256
NEAR = 512


def split(x):
    hi = x.astype(BF16)
    lo = (x - hi.astype(F32)).astype(BF16)
    return hi, lo


def dot(a, b):
    return jnp.dot(a, b, preferred_element_type=F32)


def dot_nt(a, b):
    return lax.dot_general(a, b, (((1,), (1,)), ((), ())), preferred_element_type=F32)


def column(row):
    n = row.shape[1]
    return jnp.transpose(jnp.broadcast_to(row, (8, n)))[:, 0:1]


def hot_down(row, length):
    n = row.shape[1]
    spots = lax.broadcasted_iota(jnp.int32, (length, n), 0)
    return jnp.where(spots == row, 1.0, 0.0).astype(BF16)


def hot_along(col, length, start=0):
    n = col.shape[0]
    spots = lax.broadcasted_iota(jnp.int32, (n, length), 1) + start
    return jnp.where(spots == col, 1.0, 0.0).astype(BF16)


def picked(matrix, hot):
    hi, lo = split(matrix)
    return dot(hi, hot) + dot(lo, hot)


def scores(q_t, t):
    (qa, qb), (ta, tb) = q_t, split(t)
    return dot(qa, ta) + dot(qa, tb) + dot(qb, ta)


def weights(score, target_col, negative_col, start):
    spots = lax.broadcasted_iota(jnp.int32, score.shape, 1) + start
    share = 1.0 / negative_col.shape[0]
    count = jnp.sum(jnp.where(spots == negative_col, share, 0.0), axis=0, keepdims=True)
    level = jax.nn.sigmoid(score)
    return split(level * count + jnp.where(spots == target_col, level - 1.0, 0.0))


def stepped(matrix, state, grad):
    fresh = state + jnp.sum(grad * grad, axis=0, keepdims=True) * (1.0 / grad.shape[0])
    return matrix - grad * (LR / (jnp.sqrt(fresh) + EPS)), fresh


def started(copies):
    out = [pltpu.make_async_copy(src, dst, sem) for src, dst, sem in copies]
    for c in out:
        c.start()
    return out


def near_body(bucket, s_in, t_in, tst_in, r_in, sid_in, tid_in, rid_in, nid_in,
              near_ref, src_ref, rel_ref, qa_ref, qb_ref, qta_ref, qtb_ref, wa_ref, wb_ref,
              tfar_ref, tstfar_ref, spots_ref,
              s_ref, t_ref, tst_ref, r_ref, sid_ref, tid_ref, rid_ref, nid_ref, sems):
    d, rows = s_ref.shape
    half = d // 16 * 8
    first = started([
        (sid_in, sid_ref, sems.at[0]), (rid_in, rid_ref, sems.at[1]), (r_in, r_ref, sems.at[2]),
        (s_in.at[0:half], s_ref.at[0:half], sems.at[3]), (s_in.at[half:], s_ref.at[half:], sems.at[4])])
    for c in first[0:3]:
        c.wait()
    hot_r = hot_down(rid_ref[bucket:bucket + 1, :], r_ref.shape[1])
    hot_s = hot_down(sid_ref[bucket:bucket + 1, :], rows)
    rel = picked(r_ref[...], hot_r)
    first[3].wait()
    second = started([
        (tid_in, tid_ref, sems.at[5]), (nid_in, nid_ref, sems.at[6]), (tst_in, tst_ref, sems.at[7]),
        (t_in.at[:, 0:NEAR], t_ref, sems.at[8]), (t_in.at[:, NEAR:], tfar_ref, sems.at[9])])
    upper = picked(s_ref[0:half], hot_s)
    first[4].wait()
    src = jnp.concatenate([upper, picked(s_ref[half:], hot_s)], axis=0)
    src_ref[...] = src
    rel_ref[...] = rel
    q = src * rel
    qa, qb = split(q)
    qa_ref[...] = qa
    qb_ref[...] = qb
    q_t = split(jnp.transpose(q))
    qta_ref[...], qtb_ref[...] = q_t
    for c in second[0:4]:
        c.wait()
    target_col = column(tid_ref[bucket:bucket + 1, :])
    negative_col = column(nid_ref[bucket:bucket + 1, :])
    spots_ref[:, 0:1] = target_col
    spots_ref[:, 1:2] = negative_col
    state = tst_ref[...][None]
    tstfar_ref[...] = jnp.broadcast_to(state[:, NEAR:], tstfar_ref.shape)
    later = scores(q_t, t_ref[:, 0:TILE])
    for start in range(0, NEAR, TILE):
        cols = slice(start, start + TILE)
        score = later
        if start + TILE < NEAR:
            later = scores(q_t, t_ref[:, start + TILE:start + 2 * TILE])
        wa, wb = weights(score, target_col, negative_col, start)
        wa_ref[:, cols] = wa
        wb_ref[:, cols] = wb
        t_new, fresh = stepped(t_ref[:, cols], state[:, cols], dot(qa, wa) + dot(qb, wa) + dot(qa, wb))
        near_ref[0:d, cols] = t_new
        near_ref[d:d + 8, cols] = jnp.broadcast_to(fresh, (8, TILE))
    second[4].wait()


def far_body(t_ref, tst_ref, spots_ref, qa_ref, qb_ref, qta_ref, qtb_ref,
             far_ref, up_ref, down_ref, wa_ref, wb_ref):
    d = t_ref.shape[0]
    t, qa, qb = t_ref[...], qa_ref[...], qb_ref[...]
    score = scores((qta_ref[...], qtb_ref[...]), t)
    wa, wb = weights(score, spots_ref[:, 0:1], spots_ref[:, 1:2], NEAR)
    wa_ref[...] = wa
    wb_ref[...] = wb
    t_new, fresh = stepped(t, tst_ref[0:1, :], dot(qa, wa) + dot(qb, wa) + dot(qa, wb))
    far_ref[0:d, :] = t_new
    far_ref[d:d + 8, :] = jnp.broadcast_to(fresh, (8, t.shape[1]))
    cut = up_ref.shape[1]
    up_ref[...] = far_ref[:, 0:cut]
    down_ref[...] = far_ref[:, cut:]


def source_body(bucket, s_in, sst_in, t_in, r_in, sid_in, rid_in,
                src_ref, rel_ref, wna_ref, wnb_ref, wfa_ref, wfb_ref,
                snew_out, sst_out, rel2_out, qa_out, qb_out, rgrad_ref, src2_ref, qta_ref, qtb_ref,
                s_ref, sst_ref, t_ref, r_ref, sid_ref, rid_ref,
                snew_ref, sstnew_ref, rel2_ref, qa_ref, qb_ref, sems):
    d, rows = s_ref.shape
    copies = started([
        (t_in, t_ref, sems.at[0]), (sid_in, sid_ref, sems.at[1]), (rid_in, rid_ref, sems.at[2]),
        (r_in, r_ref, sems.at[3]), (s_in, s_ref, sems.at[4]), (sst_in, sst_ref, sems.at[5])])
    copies[0].wait()
    ta, tb = split(t_ref[:, 0:NEAR])
    gq = dot_nt(ta, wna_ref[...]) + dot_nt(tb, wna_ref[...]) + dot_nt(ta, wnb_ref[...])
    ta, tb = split(t_ref[:, NEAR:])
    gq += dot_nt(ta, wfa_ref[...]) + dot_nt(tb, wfa_ref[...]) + dot_nt(ta, wfb_ref[...])
    for c in copies[1:]:
        c.wait()
    rid_col = column(rid_ref[bucket:bucket + 1, :])
    sid_col = column(sid_ref[bucket:bucket + 1, :])
    rgrad_ref[...] = picked(gq * src_ref[...], hot_along(rid_col, r_ref.shape[1]))
    grad = picked(gq * rel_ref[...], hot_along(sid_col, rows))
    s_new, fresh = stepped(s_ref[...], sst_ref[...][None], grad)
    snew_ref[...] = s_new
    sstnew_ref[...] = fresh[0]
    outs = started([(snew_ref, snew_out, sems.at[6]), (sstnew_ref, sst_out, sems.at[7])])
    after = bucket + 1
    src = picked(s_new, hot_down(sid_ref[after:after + 1, :], rows))
    rel = picked(r_ref[...], hot_down(rid_ref[after:after + 1, :], r_ref.shape[1]))
    src2_ref[...] = src
    rel2_ref[...] = rel
    q = src * rel
    qa_ref[...], qb_ref[...] = split(q)
    outs += started([(rel2_ref, rel2_out, sems.at[8]), (qa_ref, qa_out, sems.at[9]), (qb_ref, qb_out, sems.at[10])])
    qta_ref[...], qtb_ref[...] = split(jnp.transpose(q))
    for c in outs:
        c.wait()


def query_body(bucket, direct_ref, up_ref, down_ref, near_ref, src_ref, qta_ref, qtb_ref, rgrad_ref,
               tid_ref, rid_ref, nid_ref,
               gq_ref, wa_ref, wb_ref, t_out, sum_out, far_ref, sum_ref, sems):
    d = src_ref.shape[0]
    rows = wa_ref.shape[1]
    cut = up_ref.shape[1]
    far_ref[:, 0:cut] = direct_ref[:, 0:cut] + up_ref[...]
    far_ref[:, cut:] = direct_ref[:, cut:] + down_ref[...]
    outs = started([(near_ref, t_out.at[:, 0:NEAR], sems.at[0]), (far_ref, t_out.at[:, NEAR:], sems.at[1])])
    q_t = (qta_ref[...], qtb_ref[...])
    target_col = column(tid_ref[bucket:bucket + 1, :])
    negative_col = column(nid_ref[bucket:bucket + 1, :])

    def block(start):
        if start < NEAR:
            return near_ref[0:d, start:start + TILE]
        return far_ref[0:d, start - NEAR:start - NEAR + TILE]

    gq = jnp.zeros(src_ref.shape, F32)
    later = scores(q_t, block(0))
    for start in range(0, rows, TILE):
        cols = slice(start, start + TILE)
        score = later
        if start + TILE < rows:
            later = scores(q_t, block(start + TILE))
        wa, wb = weights(score, target_col, negative_col, start)
        wa_ref[:, cols] = wa
        wb_ref[:, cols] = wb
        ta, tb = split(block(start))
        gq += dot_nt(ta, wa) + dot_nt(tb, wa) + dot_nt(ta, wb)
    gq_ref[...] = gq
    rid_col = column(rid_ref[bucket:bucket + 1, :])
    sum_ref[...] = rgrad_ref[...] + picked(gq * src_ref[...], hot_along(rid_col, rgrad_ref.shape[1]))
    outs += started([(sum_ref, sum_out.at[i], sems.at[2 + i]) for i in range(sum_out.shape[0])])
    for c in outs:
        c.wait()


def target_body(t_in, qa_in, qb_in, wa_ref, wb_ref, tnew_out, tst_out,
                t_ref, qa_ref, qb_ref, tnew_ref, tst_ref, sems):
    d, rows = tnew_ref.shape
    c_a, c_b, c_t = started([(qa_in, qa_ref, sems.at[4]), (qb_in, qb_ref, sems.at[5]), (t_in, t_ref, sems.at[6])])
    c_a.wait()
    c_b.wait()
    qa, qb = qa_ref[...], qb_ref[...]
    outs = []
    for i, start in enumerate(range(0, rows, TILE)):
        cols = slice(start, start + TILE)
        wa, wb = wa_ref[:, cols], wb_ref[:, cols]
        grad = dot(qa, wa) + dot(qb, wa) + dot(qa, wb)
        if i == 0:
            c_t.wait()
        t_new, fresh = stepped(t_ref[0:d, cols], t_ref[d:d + 1, cols], grad)
        tnew_ref[:, cols] = t_new
        tst_ref[cols] = fresh[0]
        outs += started([(tnew_ref.at[:, cols], tnew_out.at[:, cols], sems.at[1 + i])])
    outs += started([(tst_ref, tst_out, sems.at[0])])
    for c in outs:
        c.wait()


def last_source_body(bucket, s_in, sst_in, gq_ref, rel_in, sid_in, snew_out, sst_out,
                     s_ref, sst_ref, rel_ref, sid_ref, snew_ref, sstnew_ref, sems):
    d, rows = s_ref.shape
    c_sid, c_rel, c_s, c_sst = started([
        (sid_in, sid_ref, sems.at[4]), (rel_in, rel_ref, sems.at[5]), (s_in, s_ref, sems.at[6]),
        (sst_in, sst_ref, sems.at[7])])
    c_sid.wait()
    c_rel.wait()
    sid_col = column(sid_ref[bucket:bucket + 1, :])
    ga, gb = split(gq_ref[...] * rel_ref[...])
    c_s.wait()
    c_sst.wait()
    outs = []
    for i, start in enumerate(range(0, rows, TILE)):
        cols = slice(start, start + TILE)
        hot = hot_along(sid_col, TILE, start)
        s_new, fresh = stepped(s_ref[:, cols], sst_ref[cols][None], dot(ga, hot) + dot(gb, hot))
        snew_ref[:, cols] = s_new
        sstnew_ref[cols] = fresh[0]
        outs += started([(snew_ref.at[:, cols], snew_out.at[:, cols], sems.at[1 + i])])
    outs += started([(sstnew_ref, sst_out, sems.at[0])])
    for c in outs:
        c.wait()


HBM, VM = pltpu.HBM, pltpu.VMEM


def call(body, ins, outs, scratch=(), flops=0):
    moved = sum(a.size * a.dtype.itemsize for _, a in (*ins, *outs))
    return pl.pallas_call(
        body,
        out_shape=[m(a.shape, a.dtype) for m, a in outs],
        in_specs=[pl.BlockSpec(memory_space=m) for m, _ in ins],
        out_specs=[pl.BlockSpec(memory_space=m) for m, _ in outs],
        scratch_shapes=list(scratch),
        compiler_params=pltpu.CompilerParams(vmem_limit_bytes=VMEM_LIMIT),
        cost_estimate=pl.CostEstimate(flops=flops, bytes_accessed=moved, transcendentals=0),
    )(*[pltpu.with_memory_space_constraint(a, m) for m, a in ins])


def of(spec, *arrays):
    return [(spec, a) for a in arrays]


def room(*arrays):
    return [pltpu.VMEM(a.shape, a.dtype) for a in arrays]


def per_device(s, sst, t, tst, r, rst, sid, tid, rid, nid):
    d, rows = s.shape
    edges = sid.shape[1]
    rels = r.shape[1]
    away = rows - NEAR
    shape = jax.ShapeDtypeStruct
    sems = pltpu.SemaphoreType.DMA((12,))
    wide = shape((d, edges), F32)
    thin = shape((d, edges), BF16)
    thin_t = shape((edges, d), BF16)
    full = shape((d, rows), F32)
    held = shape((d + 8, rows), F32)
    line = shape((rows,), F32)
    half = shape((edges, rows), BF16)
    near_w = shape((edges, NEAR), BF16)
    far_w = shape((edges, away), BF16)
    unit = 2 * d * rows * edges

    near, src0, rel0, qa0, qb0, qta0, qtb0, wna, wnb, tfar, tstfar, spots = call(
        functools.partial(near_body, 0),
        of(HBM, s, t, tst, r, sid, tid, rid, nid),
        of(VM, shape((d + 8, NEAR), F32), wide, wide, thin, thin, thin_t, thin_t,
           near_w, near_w, shape((d, away), F32), shape((8, away), F32), shape((edges, 2), jnp.int32)),
        [*room(s, shape((d, NEAR), F32), tst, r, sid, tid, rid, nid), sems], flops=7 * unit)
    cut = away // 2
    far, up, down, wfa, wfb = call(
        far_body,
        of(VM, tfar, tstfar, spots, qa0, qb0, qta0, qtb0),
        of(VM, shape((d + 8, away), F32), shape((d + 8, cut), F32), shape((d + 8, away - cut), F32), far_w, far_w),
        flops=2 * unit)

    count = lax.axis_size("blk")
    run = 16
    ring = [(i, (i + 1) % count) for i in range(count)]
    turns = [p for p in ring if p[1] % run == 0]
    near = lax.ppermute(near, "blk", ring)
    up = lax.ppermute(up, "blk", [(a, (b + run - 2) % count) for a, b in turns])
    down = lax.ppermute(down, "blk", [(a, (b + run - 4) % count) for a, b in turns])
    direct = lax.ppermute(far, "blk", [p for p in ring if p not in turns])
    s1, sst1, rel1, qa1, qb1, rgrad0, src1, qta1, qtb1 = call(
        functools.partial(source_body, 0),
        of(HBM, s, sst, t, r, sid, rid) + of(VM, src0, rel0, wna, wnb, wfa, wfb),
        of(HBM, full, line, wide, thin, thin) + of(VM, shape((d, rels), F32), wide, thin_t, thin_t),
        [*room(s, sst, t, r, sid, rid, full, line, wide, thin, thin), sems], flops=9 * unit)
    up, down, s1 = lax.optimization_barrier((up, down, s1))
    up = lax.ppermute(up, "blk", [((b + run - 2) % count, b) for a, b in turns])
    down = lax.ppermute(down, "blk", [((b + run - 4) % count, b) for a, b in turns])

    group = lax.axis_size("rel")
    gq1, wa1, wb1, t1, total = call(
        functools.partial(query_body, 1),
        of(VM, direct, up, down, near, src1, qta1, qtb1, rgrad0, tid, rid, nid),
        of(VM, wide, half, half) + of(HBM, held, shape((group, d, rels), F32)),
        [pltpu.VMEM((d + 8, away), F32), pltpu.VMEM((d, rels), F32), sems], flops=7 * unit)
    every = lax.all_to_all(total, "rel", 0, 0, tiled=True)
    t2, tst2 = call(
        target_body,
        of(HBM, t1, qa1, qb1) + of(VM, wa1, wb1),
        of(HBM, full, line),
        [*room(held, thin, thin, full, line), sems], flops=3 * unit)
    s2, sst2 = call(
        functools.partial(last_source_body, 1),
        of(HBM, s1, sst1) + of(VM, gq1) + of(HBM, rel1, sid),
        of(HBM, full, line),
        [*room(s1, sst1, rel1, sid, full, line), sems], flops=2 * unit)
    summed = every.sum(axis=0)
    rst1 = rst + summed * summed
    r1 = r - LR * summed / (jnp.sqrt(rst1) + EPS)
    return s2, sst2, t2, tst2, r1, rst1


def solution(mesh):
    both = ("blk", "rel")
    placed = (
        P(None, both), P(both), P(None, both), P(both), P(None, "blk"), P(None, "blk"),
        P(None, both), P(None, both), P(None, both), P(None, both),
    )
    return jax.shard_map(
        per_device,
        mesh=mesh,
        in_specs=placed,
        out_specs=placed[:6],
        check_vma=False,
    )
```

time: 72.3 us -> 63.7 us (0.88)
  starting transfers between devices: 21.4 us -> 14.8 us
  Pallas kernels: 31 us -> 25.3 us
  waiting for transfers between devices: 17.8 us -> 20 us
  other arithmetic: 0.84 us -> 2.37 us
    ppermute x1, waiting for transfers between devices: 15.5 us -> 1.89 us  [per_device(): near = lax.ppermute(near, 'blk', ring)]
    ppermute x2 -> x4, waiting for transfers between devices: 0.01 us -> 12.8 us  [the longest x1 12.8 us: per_device(): up = lax.ppermute(up, 'blk', [((b + run - 2) % count, b) for a, b in turns])]
    all_to_all x2 -> x1, starting transfers between devices: 13.9 us -> 5.37 us  [per_device(): every = lax.all_to_all(total, 'rel', 0, 0, tiled=True)]
    pallas_call x7 -> x6, Pallas kernels: 31 us -> 25.3 us  [call(): pl.pallas_call(body, out_shape=[m(a.shape, a.dtype) for m, a in outs], in...]
    all_to_all x2 -> x1, waiting for transfers between devices: 2.33 us -> 5.37 us  [per_device(): every = lax.all_to_all(total, 'rel', 0, 0, tiled=True)]
    ppermute x2 -> x4, starting transfers between devices: 1.98 us -> 3.93 us  [the longest x1 1.29 us: per_device(): up = lax.ppermute(up, 'blk', [((b + run - 2) % count, b) for a, b in turns])]
    reduce_sum x0 -> x1, other arithmetic: none -> 1.53 us  [per_device(): summed = every.sum(axis=0)]
  transfers between devices with their start and end apart: 6 -> 7, of which waited for: 3 -> 3; matrix products, arithmetic and copies ran while one was open for 0% -> 0% of each run, Pallas kernels for 25% -> 24%
where the time goes in v2:
time: 63.7 us; the launch traced here: 63.4 us
  Pallas kernels  25.3 us (40%)
  waiting for transfers between devices  20 us (31%)
  starting transfers between devices  14.8 us (23%)
  other arithmetic  2.37 us (4%)
  between operations  0.82 us (1%)
    pallas_call x6, Pallas kernels, call(): pl.pallas_call(body, out_shape=[m(a.shape, a.dtype) for m, a in outs], in...  25.3 us
    ppermute x1, waiting for transfers between devices, per_device(): up = lax.ppermute(up, 'blk', [((b + run - 2) % count, b) for a, b in turns])  12.8 us
    all_to_all x1, waiting for transfers between devices, per_device(): every = lax.all_to_all(total, 'rel', 0, 0, tiled=True)  5.37 us
    all_to_all x1, starting transfers between devices, per_device(): every = lax.all_to_all(total, 'rel', 0, 0, tiled=True)  5.37 us
    ppermute x1, starting transfers between devices, per_device(): direct = lax.ppermute(far, 'blk', [p for p in ring if p not in turns])  3.61 us
    ppermute x1, starting transfers between devices, per_device(): near = lax.ppermute(near, 'blk', ring)  1.92 us
    ppermute x1, waiting for transfers between devices, per_device(): near = lax.ppermute(near, 'blk', ring)  1.89 us
    reduce_sum x1, other arithmetic, per_device(): summed = every.sum(axis=0)  1.53 us
  transfers between devices with their start and end apart: 7, of which 3 were waited for; matrix products, arithmetic and copies ran while one was open for 0% of the time, Pallas kernels for 24%

profile of v2, /device:TPU:2, one launch (start us, length us, event | category | flops | bytes accessed | tf_op | source)
XLA Modules:
  0.0 63.4 jit_solution(12429258304696400715)
XLA Ops:
  0.6 5.2 %shard_map.145 = (f32[408,512]{1,0:T(8,128)S(1)}, f32[400,512]{1,0:T(8,128)S(1)}, f32[400,512]{1,0:T(8,128)S(1)}, bf16[400,512]{1,0:T(8,128)(2,1)S(1)}, bf16[400...) custom-call(f32[400,768]{1,0:T(8,128)} %s_in.3, ...), custom_call_target="tpu_custom_call" | custom-call | flops 2202009600 | bytes 8264704 | tf_op jit(solution)/shard_map/pallas_call | solution.py:276
  5.8 1.9 %collective-permute-start.5 = (f32[408,512]{1,0:T(8,128)S(1)}, f32[408,512]{1,0:T(8,128)S(1)}, u32[]{:S(2)}, u32[]{:S(2)}) collective-permute-start(f32[408,512]{1,0:T(8,128)S(1)} %get-tuple-element.65), channel_id=1, source_target_pairs={{0,8},{8,16},{16,24},{24,32},{32,40},{40,48},{48,56},{56,64},{64,7... | collective-permute-start | bytes 2506760 | tf_op jit(solution)/shard_map/ppermute | solution.py:330
  7.8 1.7 %shard_map.146 = (f32[408,256]{1,0:T(8,128)S(1)}, f32[408,128]{1,0:T(8,128)S(1)}, f32[408,128]{1,0:T(8,128)S(1)}, bf16[512,256]{1,0:T(8,128)(2,1)S(1)}, bf16[512,256]{1,0:T(8,128)(2,1)S(1)}) custom-call(f32[400,256]{1,0:T(8,128)S(1)} %get-tuple-element.44.t_ref, f32[8,256]{1,0:T(8,128)S(1)} %get-tuple-element.45.tst_ref, ...), custom_call_target="tpu_custom_call" | custom-call | flops 629145600 | bytes 3420160 | tf_op jit(solution)/shard_map/pallas_call | solution.py:276
  9.5 0.7 %collective-permute-start = (f32[408,128]{1,0:T(8,128)S(1)}, f32[408,128]{1,0:T(8,128)S(1)}, u32[]{:S(2)}, u32[]{:S(2)}) collective-permute-start(f32[408,128]{1,0:T(8,128)S(1)} %get-tuple-element.51), channel_id=1, source_target_pairs={{120,240},{248,368},{376,496},{504,112},{121,241},{249,369},{377,4... | collective-permute-start | bytes 626696 | tf_op jit(solution)/shard_map/ppermute | solution.py:331
  10.2 0.7 %collective-permute-start.1 = (f32[408,128]{1,0:T(8,128)S(1)}, f32[408,128]{1,0:T(8,128)S(1)}, u32[]{:S(2)}, u32[]{:S(2)}) collective-permute-start(f32[408,128]{1,0:T(8,128)S(1)} %get-tuple-element.52), channel_id=1, source_target_pairs={{120,224},{248,352},{376,480},{504,96},{121,225},{249,353},{377,48... | collective-permute-start | bytes 626696 | tf_op jit(solution)/shard_map/ppermute | solution.py:332
  10.8 3.6 %collective-permute-start.2 = (f32[408,256]{1,0:T(8,128)S(1)}, f32[408,256]{1,0:T(8,128)S(1)}, u32[]{:S(2)}, u32[]{:S(2)}) collective-permute-start(f32[408,256]{1,0:T(8,128)S(1)} %get-tuple-element.62), channel_id=1, source_target_pairs={{0,8},{8,16},{16,24},{24,32},{32,40},{40,48},{48,56},{56,64},{64,7... | collective-permute-start | bytes 1253384 | tf_op jit(solution)/shard_map/ppermute | solution.py:333
  14.5 0.0 copy-start
  14.5 0.0 copy-start.1
  14.5 0.0 copy-start.2
  14.5 6.5 %shard_map.147 = (f32[400,768]{1,0:T(8,128)}, f32[768]{0:T(1024)}, f32[400,512]{1,0:T(8,128)}, bf16[400,512]{1,0:T(8,128)(2,1)}, bf16[400,512]{1,0:T(8,128)(2,1)...) custom-call(f32[400,768]{1,0:T(8,128)} %s_in.3, ...), custom_call_target="tpu_custom_call" | custom-call | flops 2831155200 | bytes 10598400 | tf_op jit(solution)/shard_map/pallas_call | solution.py:276
  21.0 0.0 collective-permute-done
  21.0 0.0 collective-permute-done.1
  21.0 1.3 %collective-permute-start.3 = (f32[408,128]{1,0:T(8,128)S(1)}, f32[408,128]{1,0:T(8,128)S(1)}, u32[]{:S(2)}, u32[]{:S(2)}) collective-permute-start(f32[408,128]{1,0:T(8,128)S(1)} %collective-permute-done), channel_id=1, source_target_pairs={{240,128},{368,256},{496,384},{112,0},{241,129},{369,257},{497,385... | collective-permute-start | bytes 626696 | tf_op jit(solution)/shard_map/ppermute | solution.py:340
  22.3 1.3 %collective-permute-start.4 = (f32[408,128]{1,0:T(8,128)S(1)}, f32[408,128]{1,0:T(8,128)S(1)}, u32[]{:S(2)}, u32[]{:S(2)}) collective-permute-start(f32[408,128]{1,0:T(8,128)S(1)} %collective-permute-done.1), channel_id=1, source_target_pairs={{224,128},{352,256},{480,384},{96,0},{225,129},{353,257},{481,385}... | collective-permute-start | bytes 626696 | tf_op jit(solution)/shard_map/ppermute | solution.py:341
  23.6 0.0 collective-permute-done.2.direct_ref
  23.6 12.8 %collective-permute-done.3.up_ref = f32[408,128]{1,0:T(8,128)S(1)} collective-permute-done((f32[408,128]{1,0:T(8,128)S(1)}, f32[408,128]{1,0:T(8,128)S(1)}, u32[]{:S(2)}, u32[]{:S(2)}) %collective-permute-start.3) | collective-permute-done | bytes 208928 | tf_op jit(solution)/shard_map/ppermute | solution.py:340
  36.4 0.0 collective-permute-done.4.down_ref
  36.4 1.9 %collective-permute-done.5.near_ref = f32[408,512]{1,0:T(8,128)S(1)} collective-permute-done((f32[408,512]{1,0:T(8,128)S(1)}, f32[408,512]{1,0:T(8,128)S(1)}, u32[]{:S(2)}, u32[]{:S(2)}) %collective-permute-start.5) | collective-permute-done | bytes 835616 | tf_op jit(solution)/shard_map/ppermute | solution.py:330
  38.2 0.0 copy-done
  38.3 0.0 copy-done.1
  38.3 0.0 copy-done.2
  38.3 4.6 %shard_map.148 = (f32[400,512]{1,0:T(8,128)S(1)}, bf16[512,768]{1,0:T(8,128)(2,1)S(1)}, bf16[512,768]{1,0:T(8,128)(2,1)S(1)}, f32[408,768]{1,0:T(8,128)}, f32[8,400,128]{2,1,0:T(8,128)}) custom-call(f32[408,256]{1,0:T(8,128)S(1)} %collective-permute-done.2.direct_ref, f32[408,128]{1,0:T(8,128)S(1)} %collective-permute-done.3.up_ref, ...), custom_call_target="tpu_custom_call" | custom-call | flops 2202009600 | bytes 8810496 | tf_op jit(solution)/shard_map/pallas_call | solution.py:276
  42.9 5.4 %all-to-all-start = ((f32[8,400,128]{2,1,0:T(8,128)}), f32[8,400,128]{2,1,0:T(8,128)}, u32[]{:S(2)}, u32[]{:S(2)}) async-start(f32[8,400,128]{2,1,0:T(8,128)} %get-tuple-element.81), calls=%async_computation | async-start | bytes 3276800 | tf_op jit(solution)/shard_map/all_to_all | solution.py:349
  48.3 3.6 %shard_map.149 = (f32[400,768]{1,0:T(8,128)}, f32[768]{0:T(1024)}) custom-call(f32[400,768]{1,0:T(8,128)} %get-tuple-element.60.s_in, f32[768]{0:T(1024)} %get-tuple-element.61.sst_in, f32[400,512]{1,0:T(8,128)S(1)} %get-tuple-element.70.gq_ref, f32[400,512]{1,0:T(8,128)} %get-tuple-element.71.rel_in, s32[2,512]{1,0:T(2,128)} %sid_in.5), custom_call_target="tpu_custom_call" | custom-call | flops 629145600 | bytes 4106240 | tf_op jit(solution)/shard_map/pallas_call | solution.py:276
  51.8 3.7 %shard_map.150 = (f32[400,768]{1,0:T(8,128)}, f32[768]{0:T(1024)}) custom-call(f32[408,768]{1,0:T(8,128)} %get-tuple-element.74.t_in, bf16[400,512]{1,0:T(8,128)(2,1)} %get-tuple-element.75.qa_in, bf16[400,512]{1,0:T(8,128)(2,1)} %get-tuple-element.76.qb_in, bf16[512,768]{1,0:T(8,128)(2,1)S(1)} %get-tuple-element.77.wa_ref, ...), custom_call_target="tpu_custom_call" | custom-call | flops 943718400 | bytes 4877312 | tf_op jit(solution)/shard_map/pallas_call | solution.py:276
  55.6 0.0 copy-start.3
  55.6 0.0 copy-start.4
  55.6 5.4 %all-to-all-done = f32[8,400,128]{2,1,0:T(8,128)} async-done(((f32[8,400,128]{2,1,0:T(8,128)}), f32[8,400,128]{2,1,0:T(8,128)}, u32[]{:S(2)}, u32[]{:S(2)}) %all-to-all-start) | async-done | bytes 1638432 | tf_op jit(solution)/shard_map/all_to_all | solution.py:349
  61.0 1.5 %reduce_sum.9 = f32[400,128]{1,0:T(8,128)S(1)} reduce(f32[8,400,128]{2,1,0:T(8,128)} %all-to-all-done, f32[]{:T(128)} %constant.0.clone.1), dimensions={0}, to_apply=%region_0.0 | reduce | flops 358400 | bytes 1843204 | tf_op jit(solution)/shard_map/reduce_sum | solution.py:360
  62.5 0.0 copy-done.3
  62.5 0.0 copy-done.4
  62.5 0.8 %divide_subtract_fusion = (f32[400,128]{1,0:T(8,128)}, f32[400,128]{1,0:T(8,128)}) fusion(f32[400,128]{1,0:T(8,128)S(1)} %copy-done.3, f32[400,128]{1,0:T(8,128)S(1)} %reduce_sum.9, f32[400,128]{1,0:T(8,128)S(1)} %copy-done.4), kind=kLoop, calls=%fused_computation | loop fusion | flops 307200 | bytes 1024000 | tf_op jit(solution)/shard_map/sub | solution.py:362
Async XLA Ops:
  5.8 32.4 %collective-permute-start.5 = (f32[408,512]{1,0:T(8,128)S(1)}, f32[408,512]{1,0:T(8,128)S(1)}, u32[]{:S(2)}, u32[]{:S(2)}) collective-permute-start(f32[408,512]{1,0:T(8,128)S(1)} %get-tuple-element.65), channel_id=1, source_target_pairs={{0,8},{8,16},{16,24},{24,32},{32,40},{40,48},{48,56},{56,64},{64,7... | collective-permute-start | bytes 2506760 | tf_op jit(solution)/shard_map/ppermute | solution.py:330
  9.5 11.5 %collective-permute-start = (f32[408,128]{1,0:T(8,128)S(1)}, f32[408,128]{1,0:T(8,128)S(1)}, u32[]{:S(2)}, u32[]{:S(2)}) collective-permute-start(f32[408,128]{1,0:T(8,128)S(1)} %get-tuple-element.51), channel_id=1, source_target_pairs={{120,240},{248,368},{376,496},{504,112},{121,241},{249,369},{377,4... | collective-permute-start | bytes 626696 | tf_op jit(solution)/shard_map/ppermute | solution.py:331
  10.2 10.8 %collective-permute-start.1 = (f32[408,128]{1,0:T(8,128)S(1)}, f32[408,128]{1,0:T(8,128)S(1)}, u32[]{:S(2)}, u32[]{:S(2)}) collective-permute-start(f32[408,128]{1,0:T(8,128)S(1)} %get-tuple-element.52), channel_id=1, source_target_pairs={{120,224},{248,352},{376,480},{504,96},{121,225},{249,353},{377,48... | collective-permute-start | bytes 626696 | tf_op jit(solution)/shard_map/ppermute | solution.py:332
  10.8 12.7 %collective-permute-start.2 = (f32[408,256]{1,0:T(8,128)S(1)}, f32[408,256]{1,0:T(8,128)S(1)}, u32[]{:S(2)}, u32[]{:S(2)}) collective-permute-start(f32[408,256]{1,0:T(8,128)S(1)} %get-tuple-element.62), channel_id=1, source_target_pairs={{0,8},{8,16},{16,24},{24,32},{32,40},{40,48},{48,56},{56,64},{64,7... | collective-permute-start | bytes 1253384 | tf_op jit(solution)/shard_map/ppermute | solution.py:333
  14.5 23.8 %copy-start = (s32[2,512]{1,0:T(2,128)S(1)}, s32[2,512]{1,0:T(2,128)}, u32[]{:S(2)}) copy-start(s32[2,512]{1,0:T(2,128)} %rid_ref.1) | copy-start | bytes 12292
  14.5 23.8 %copy-start.1 = (s32[2,512]{1,0:T(2,128)S(1)}, s32[2,512]{1,0:T(2,128)}, u32[]{:S(2)}) copy-start(s32[2,512]{1,0:T(2,128)} %tid_ref.1) | copy-start | bytes 12292
  14.5 23.8 %copy-start.2 = (s32[2,512]{1,0:T(2,128)S(1)}, s32[2,512]{1,0:T(2,128)}, u32[]{:S(2)}) copy-start(s32[2,512]{1,0:T(2,128)} %nid_ref.1) | copy-start | bytes 12292
  21.0 15.4 %collective-permute-start.3 = (f32[408,128]{1,0:T(8,128)S(1)}, f32[408,128]{1,0:T(8,128)S(1)}, u32[]{:S(2)}, u32[]{:S(2)}) collective-permute-start(f32[408,128]{1,0:T(8,128)S(1)} %collective-permute-done), channel_id=1, source_target_pairs={{240,128},{368,256},{496,384},{112,0},{241,129},{369,257},{497,385... | collective-permute-start | bytes 626696 | tf_op jit(solution)/shard_map/ppermute | solution.py:340
  22.3 14.1 %collective-permute-start.4 = (f32[408,128]{1,0:T(8,128)S(1)}, f32[408,128]{1,0:T(8,128)S(1)}, u32[]{:S(2)}, u32[]{:S(2)}) collective-permute-start(f32[408,128]{1,0:T(8,128)S(1)} %collective-permute-done.1), channel_id=1, source_target_pairs={{224,128},{352,256},{480,384},{96,0},{225,129},{353,257},{481,385}... | collective-permute-start | bytes 626696 | tf_op jit(solution)/shard_map/ppermute | solution.py:341
  42.9 18.1 %all-to-all-start = ((f32[8,400,128]{2,1,0:T(8,128)}), f32[8,400,128]{2,1,0:T(8,128)}, u32[]{:S(2)}, u32[]{:S(2)}) async-start(f32[8,400,128]{2,1,0:T(8,128)} %get-tuple-element.81), calls=%async_computation | async-start | bytes 3276800 | tf_op jit(solution)/shard_map/all_to_all | solution.py:349
  55.6 6.9 %copy-start.3 = (f32[400,128]{1,0:T(8,128)S(1)}, f32[400,128]{1,0:T(8,128)}, u32[]{:S(2)}) copy-start(f32[400,128]{1,0:T(8,128)} %r_in.3) | copy-start | bytes 614404
  55.6 6.9 %copy-start.4 = (f32[400,128]{1,0:T(8,128)S(1)}, f32[400,128]{1,0:T(8,128)}, u32[]{:S(2)}) copy-start(f32[400,128]{1,0:T(8,128)} %param.15) | copy-start | bytes 614404

commit v3 on v2

--- a/solution.py
+++ b/solution.py
@@ -82,10 +82,9 @@
               tfar_ref, tstfar_ref, spots_ref,
               s_ref, t_ref, tst_ref, r_ref, sid_ref, tid_ref, rid_ref, nid_ref, sems):
     d, rows = s_ref.shape
-    half = d // 16 * 8
     first = started([
         (sid_in, sid_ref, sems.at[0]), (rid_in, rid_ref, sems.at[1]), (r_in, r_ref, sems.at[2]),
-        (s_in.at[0:half], s_ref.at[0:half], sems.at[3]), (s_in.at[half:], s_ref.at[half:], sems.at[4])])
+        (s_in, s_ref, sems.at[3])])
     for c in first[0:3]:
         c.wait()
     hot_r = hot_down(rid_ref[bucket:bucket + 1, :], r_ref.shape[1])
@@ -95,9 +94,7 @@
     second = started([
         (tid_in, tid_ref, sems.at[5]), (nid_in, nid_ref, sems.at[6]), (tst_in, tst_ref, sems.at[7]),
         (t_in.at[:, 0:NEAR], t_ref, sems.at[8]), (t_in.at[:, NEAR:], tfar_ref, sems.at[9])])
-    upper = picked(s_ref[0:half], hot_s)
-    first[4].wait()
-    src = jnp.concatenate([upper, picked(s_ref[half:], hot_s)], axis=0)
+    src = picked(s_ref[...], hot_s)
     src_ref[...] = src
     rel_ref[...] = rel
     q = src * rel

time: 63.7 us -> 64.6 us (1.014)
  Pallas kernels: 25.3 us -> 26.1 us
    pallas_call x6, Pallas kernels: 25.3 us -> 26.1 us  [call(): pl.pallas_call(body, out_shape=[m(a.shape, a.dtype) for m, a in outs], in...]
where the time goes in v3:
time: 64.6 us; the launch traced here: 64.2 us
  Pallas kernels  26.1 us (40%)
  waiting for transfers between devices  20 us (31%)
  starting transfers between devices  14.8 us (23%)
  other arithmetic  2.37 us (4%)
  between operations  0.82 us (1%)
    pallas_call x6, Pallas kernels, call(): pl.pallas_call(body, out_shape=[m(a.shape, a.dtype) for m, a in outs], in...  26.1 us
    ppermute x1, waiting for transfers between devices, per_device(): up = lax.ppermute(up, 'blk', [((b + run - 2) % count, b) for a, b in turns])  12.8 us
    all_to_all x1, waiting for transfers between devices, per_device(): every = lax.all_to_all(total, 'rel', 0, 0, tiled=True)  5.37 us
    all_to_all x1, starting transfers between devices, per_device(): every = lax.all_to_all(total, 'rel', 0, 0, tiled=True)  5.36 us
    ppermute x1, starting transfers between devices, per_device(): direct = lax.ppermute(far, 'blk', [p for p in ring if p not in turns])  3.6 us
    ppermute x1, starting transfers between devices, per_device(): near = lax.ppermute(near, 'blk', ring)  1.92 us
    ppermute x1, waiting for transfers between devices, per_device(): near = lax.ppermute(near, 'blk', ring)  1.88 us
    reduce_sum x1, other arithmetic, per_device(): summed = every.sum(axis=0)  1.53 us
  transfers between devices with their start and end apart: 7, of which 3 were waited for; matrix products, arithmetic and copies ran while one was open for 0% of the time, Pallas kernels for 24%

profile of v3, /device:TPU:2, one launch (start us, length us, event | category | flops | bytes accessed | tf_op | source)
XLA Modules:
  0.0 64.2 jit_solution(2217437098381136154)
XLA Ops:
  0.6 6.0 %shard_map.145 = (f32[408,512]{1,0:T(8,128)S(1)}, f32[400,512]{1,0:T(8,128)S(1)}, f32[400,512]{1,0:T(8,128)S(1)}, bf16[400,512]{1,0:T(8,128)(2,1)S(1)}, bf16[400...) custom-call(f32[400,768]{1,0:T(8,128)} %s_in.3, ...), custom_call_target="tpu_custom_call" | custom-call | flops 2202009600 | bytes 8264704 | tf_op jit(solution)/shard_map/pallas_call | solution.py:273
  6.6 1.9 %collective-permute-start.5 = (f32[408,512]{1,0:T(8,128)S(1)}, f32[408,512]{1,0:T(8,128)S(1)}, u32[]{:S(2)}, u32[]{:S(2)}) collective-permute-start(f32[408,512]{1,0:T(8,128)S(1)} %get-tuple-element.65), channel_id=1, source_target_pairs={{0,8},{8,16},{16,24},{24,32},{32,40},{40,48},{48,56},{56,64},{64,7... | collective-permute-start | bytes 2506760 | tf_op jit(solution)/shard_map/ppermute | solution.py:327
  8.5 1.7 %shard_map.146 = (f32[408,256]{1,0:T(8,128)S(1)}, f32[408,128]{1,0:T(8,128)S(1)}, f32[408,128]{1,0:T(8,128)S(1)}, bf16[512,256]{1,0:T(8,128)(2,1)S(1)}, bf16[512,256]{1,0:T(8,128)(2,1)S(1)}) custom-call(f32[400,256]{1,0:T(8,128)S(1)} %get-tuple-element.44.t_ref, f32[8,256]{1,0:T(8,128)S(1)} %get-tuple-element.45.tst_ref, ...), custom_call_target="tpu_custom_call" | custom-call | flops 629145600 | bytes 3420160 | tf_op jit(solution)/shard_map/pallas_call | solution.py:273
  10.3 0.7 %collective-permute-start = (f32[408,128]{1,0:T(8,128)S(1)}, f32[408,128]{1,0:T(8,128)S(1)}, u32[]{:S(2)}, u32[]{:S(2)}) collective-permute-start(f32[408,128]{1,0:T(8,128)S(1)} %get-tuple-element.51), channel_id=1, source_target_pairs={{120,240},{248,368},{376,496},{504,112},{121,241},{249,369},{377,4... | collective-permute-start | bytes 626696 | tf_op jit(solution)/shard_map/ppermute | solution.py:328
  11.0 0.7 %collective-permute-start.1 = (f32[408,128]{1,0:T(8,128)S(1)}, f32[408,128]{1,0:T(8,128)S(1)}, u32[]{:S(2)}, u32[]{:S(2)}) collective-permute-start(f32[408,128]{1,0:T(8,128)S(1)} %get-tuple-element.52), channel_id=1, source_target_pairs={{120,224},{248,352},{376,480},{504,96},{121,225},{249,353},{377,48... | collective-permute-start | bytes 626696 | tf_op jit(solution)/shard_map/ppermute | solution.py:329
  11.6 3.6 %collective-permute-start.2 = (f32[408,256]{1,0:T(8,128)S(1)}, f32[408,256]{1,0:T(8,128)S(1)}, u32[]{:S(2)}, u32[]{:S(2)}) collective-permute-start(f32[408,256]{1,0:T(8,128)S(1)} %get-tuple-element.62), channel_id=1, source_target_pairs={{0,8},{8,16},{16,24},{24,32},{32,40},{40,48},{48,56},{56,64},{64,7... | collective-permute-start | bytes 1253384 | tf_op jit(solution)/shard_map/ppermute | solution.py:330
  15.3 0.0 copy-start
  15.3 0.0 copy-start.1
  15.3 0.0 copy-start.2
  15.3 6.5 %shard_map.147 = (f32[400,768]{1,0:T(8,128)}, f32[768]{0:T(1024)}, f32[400,512]{1,0:T(8,128)}, bf16[400,512]{1,0:T(8,128)(2,1)}, bf16[400,512]{1,0:T(8,128)(2,1)...) custom-call(f32[400,768]{1,0:T(8,128)} %s_in.3, ...), custom_call_target="tpu_custom_call" | custom-call | flops 2831155200 | bytes 10598400 | tf_op jit(solution)/shard_map/pallas_call | solution.py:273
  21.8 0.0 collective-permute-done
  21.8 0.0 collective-permute-done.1
  21.8 1.3 %collective-permute-start.3 = (f32[408,128]{1,0:T(8,128)S(1)}, f32[408,128]{1,0:T(8,128)S(1)}, u32[]{:S(2)}, u32[]{:S(2)}) collective-permute-start(f32[408,128]{1,0:T(8,128)S(1)} %collective-permute-done), channel_id=1, source_target_pairs={{240,128},{368,256},{496,384},{112,0},{241,129},{369,257},{497,385... | collective-permute-start | bytes 626696 | tf_op jit(solution)/shard_map/ppermute | solution.py:337
  23.1 1.3 %collective-permute-start.4 = (f32[408,128]{1,0:T(8,128)S(1)}, f32[408,128]{1,0:T(8,128)S(1)}, u32[]{:S(2)}, u32[]{:S(2)}) collective-permute-start(f32[408,128]{1,0:T(8,128)S(1)} %collective-permute-done.1), channel_id=1, source_target_pairs={{224,128},{352,256},{480,384},{96,0},{225,129},{353,257},{481,385}... | collective-permute-start | bytes 626696 | tf_op jit(solution)/shard_map/ppermute | solution.py:338
  24.4 0.0 collective-permute-done.2.direct_ref
  24.4 12.8 %collective-permute-done.3.up_ref = f32[408,128]{1,0:T(8,128)S(1)} collective-permute-done((f32[408,128]{1,0:T(8,128)S(1)}, f32[408,128]{1,0:T(8,128)S(1)}, u32[]{:S(2)}, u32[]{:S(2)}) %collective-permute-start.3) | collective-permute-done | bytes 208928 | tf_op jit(solution)/shard_map/ppermute | solution.py:337
  37.2 0.0 collective-permute-done.4.down_ref
  37.2 1.9 %collective-permute-done.5.near_ref = f32[408,512]{1,0:T(8,128)S(1)} collective-permute-done((f32[408,512]{1,0:T(8,128)S(1)}, f32[408,512]{1,0:T(8,128)S(1)}, u32[]{:S(2)}, u32[]{:S(2)}) %collective-permute-start.5) | collective-permute-done | bytes 835616 | tf_op jit(solution)/shard_map/ppermute | solution.py:327
  39.0 0.0 copy-done
  39.1 0.0 copy-done.1
  39.1 0.0 copy-done.2
  39.1 4.6 %shard_map.148 = (f32[400,512]{1,0:T(8,128)S(1)}, bf16[512,768]{1,0:T(8,128)(2,1)S(1)}, bf16[512,768]{1,0:T(8,128)(2,1)S(1)}, f32[408,768]{1,0:T(8,128)}, f32[8,400,128]{2,1,0:T(8,128)}) custom-call(f32[408,256]{1,0:T(8,128)S(1)} %collective-permute-done.2.direct_ref, f32[408,128]{1,0:T(8,128)S(1)} %collective-permute-done.3.up_ref, ...), custom_call_target="tpu_custom_call" | custom-call | flops 2202009600 | bytes 8810496 | tf_op jit(solution)/shard_map/pallas_call | solution.py:273
  43.7 5.4 %all-to-all-start = ((f32[8,400,128]{2,1,0:T(8,128)}), f32[8,400,128]{2,1,0:T(8,128)}, u32[]{:S(2)}, u32[]{:S(2)}) async-start(f32[8,400,128]{2,1,0:T(8,128)} %get-tuple-element.81), calls=%async_computation | async-start | bytes 3276800 | tf_op jit(solution)/shard_map/all_to_all | solution.py:346
  49.1 3.6 %shard_map.149 = (f32[400,768]{1,0:T(8,128)}, f32[768]{0:T(1024)}) custom-call(f32[400,768]{1,0:T(8,128)} %get-tuple-element.60.s_in, f32[768]{0:T(1024)} %get-tuple-element.61.sst_in, f32[400,512]{1,0:T(8,128)S(1)} %get-tuple-element.70.gq_ref, f32[400,512]{1,0:T(8,128)} %get-tuple-element.71.rel_in, s32[2,512]{1,0:T(2,128)} %sid_in.5), custom_call_target="tpu_custom_call" | custom-call | flops 629145600 | bytes 4106240 | tf_op jit(solution)/shard_map/pallas_call | solution.py:273
  52.6 3.7 %shard_map.150 = (f32[400,768]{1,0:T(8,128)}, f32[768]{0:T(1024)}) custom-call(f32[408,768]{1,0:T(8,128)} %get-tuple-element.74.t_in, bf16[400,512]{1,0:T(8,128)(2,1)} %get-tuple-element.75.qa_in, bf16[400,512]{1,0:T(8,128)(2,1)} %get-tuple-element.76.qb_in, bf16[512,768]{1,0:T(8,128)(2,1)S(1)} %get-tuple-element.77.wa_ref, ...), custom_call_target="tpu_custom_call" | custom-call | flops 943718400 | bytes 4877312 | tf_op jit(solution)/shard_map/pallas_call | solution.py:273
  56.4 0.0 copy-start.3
  56.4 0.0 copy-start.4
  56.4 5.4 %all-to-all-done = f32[8,400,128]{2,1,0:T(8,128)} async-done(((f32[8,400,128]{2,1,0:T(8,128)}), f32[8,400,128]{2,1,0:T(8,128)}, u32[]{:S(2)}, u32[]{:S(2)}) %all-to-all-start) | async-done | bytes 1638432 | tf_op jit(solution)/shard_map/all_to_all | solution.py:346
  61.8 1.5 %reduce_sum.9 = f32[400,128]{1,0:T(8,128)S(1)} reduce(f32[8,400,128]{2,1,0:T(8,128)} %all-to-all-done, f32[]{:T(128)} %constant.0.clone.1), dimensions={0}, to_apply=%region_0.0 | reduce | flops 358400 | bytes 1843204 | tf_op jit(solution)/shard_map/reduce_sum | solution.py:357
  63.3 0.0 copy-done.3
  63.3 0.0 copy-done.4
  63.3 0.8 %divide_subtract_fusion = (f32[400,128]{1,0:T(8,128)}, f32[400,128]{1,0:T(8,128)}) fusion(f32[400,128]{1,0:T(8,128)S(1)} %copy-done.3, f32[400,128]{1,0:T(8,128)S(1)} %reduce_sum.9, f32[400,128]{1,0:T(8,128)S(1)} %copy-done.4), kind=kLoop, calls=%fused_computation | loop fusion | flops 307200 | bytes 1024000 | tf_op jit(solution)/shard_map/sub | solution.py:359
Async XLA Ops:
  6.6 32.4 %collective-permute-start.5 = (f32[408,512]{1,0:T(8,128)S(1)}, f32[408,512]{1,0:T(8,128)S(1)}, u32[]{:S(2)}, u32[]{:S(2)}) collective-permute-start(f32[408,512]{1,0:T(8,128)S(1)} %get-tuple-element.65), channel_id=1, source_target_pairs={{0,8},{8,16},{16,24},{24,32},{32,40},{40,48},{48,56},{56,64},{64,7... | collective-permute-start | bytes 2506760 | tf_op jit(solution)/shard_map/ppermute | solution.py:327
  10.3 11.5 %collective-permute-start = (f32[408,128]{1,0:T(8,128)S(1)}, f32[408,128]{1,0:T(8,128)S(1)}, u32[]{:S(2)}, u32[]{:S(2)}) collective-permute-start(f32[408,128]{1,0:T(8,128)S(1)} %get-tuple-element.51), channel_id=1, source_target_pairs={{120,240},{248,368},{376,496},{504,112},{121,241},{249,369},{377,4... | collective-permute-start | bytes 626696 | tf_op jit(solution)/shard_map/ppermute | solution.py:328
  11.0 10.8 %collective-permute-start.1 = (f32[408,128]{1,0:T(8,128)S(1)}, f32[408,128]{1,0:T(8,128)S(1)}, u32[]{:S(2)}, u32[]{:S(2)}) collective-permute-start(f32[408,128]{1,0:T(8,128)S(1)} %get-tuple-element.52), channel_id=1, source_target_pairs={{120,224},{248,352},{376,480},{504,96},{121,225},{249,353},{377,48... | collective-permute-start | bytes 626696 | tf_op jit(solution)/shard_map/ppermute | solution.py:329
  11.6 12.7 %collective-permute-start.2 = (f32[408,256]{1,0:T(8,128)S(1)}, f32[408,256]{1,0:T(8,128)S(1)}, u32[]{:S(2)}, u32[]{:S(2)}) collective-permute-start(f32[408,256]{1,0:T(8,128)S(1)} %get-tuple-element.62), channel_id=1, source_target_pairs={{0,8},{8,16},{16,24},{24,32},{32,40},{40,48},{48,56},{56,64},{64,7... | collective-permute-start | bytes 1253384 | tf_op jit(solution)/shard_map/ppermute | solution.py:330
  15.3 23.8 %copy-start = (s32[2,512]{1,0:T(2,128)S(1)}, s32[2,512]{1,0:T(2,128)}, u32[]{:S(2)}) copy-start(s32[2,512]{1,0:T(2,128)} %rid_ref.1) | copy-start | bytes 12292
  15.3 23.8 %copy-start.1 = (s32[2,512]{1,0:T(2,128)S(1)}, s32[2,512]{1,0:T(2,128)}, u32[]{:S(2)}) copy-start(s32[2,512]{1,0:T(2,128)} %tid_ref.1) | copy-start | bytes 12292
  15.3 23.8 %copy-start.2 = (s32[2,512]{1,0:T(2,128)S(1)}, s32[2,512]{1,0:T(2,128)}, u32[]{:S(2)}) copy-start(s32[2,512]{1,0:T(2,128)} %nid_ref.1) | copy-start | bytes 12292
  21.8 15.4 %collective-permute-start.3 = (f32[408,128]{1,0:T(8,128)S(1)}, f32[408,128]{1,0:T(8,128)S(1)}, u32[]{:S(2)}, u32[]{:S(2)}) collective-permute-start(f32[408,128]{1,0:T(8,128)S(1)} %collective-permute-done), channel_id=1, source_target_pairs={{240,128},{368,256},{496,384},{112,0},{241,129},{369,257},{497,385... | collective-permute-start | bytes 626696 | tf_op jit(solution)/shard_map/ppermute | solution.py:337
  23.1 14.1 %collective-permute-start.4 = (f32[408,128]{1,0:T(8,128)S(1)}, f32[408,128]{1,0:T(8,128)S(1)}, u32[]{:S(2)}, u32[]{:S(2)}) collective-permute-start(f32[408,128]{1,0:T(8,128)S(1)} %collective-permute-done.1), channel_id=1, source_target_pairs={{224,128},{352,256},{480,384},{96,0},{225,129},{353,257},{481,385}... | collective-permute-start | bytes 626696 | tf_op jit(solution)/shard_map/ppermute | solution.py:338
  43.7 18.1 %all-to-all-start = ((f32[8,400,128]{2,1,0:T(8,128)}), f32[8,400,128]{2,1,0:T(8,128)}, u32[]{:S(2)}, u32[]{:S(2)}) async-start(f32[8,400,128]{2,1,0:T(8,128)} %get-tuple-element.81), calls=%async_computation | async-start | bytes 3276800 | tf_op jit(solution)/shard_map/all_to_all | solution.py:346
  56.4 6.9 %copy-start.3 = (f32[400,128]{1,0:T(8,128)S(1)}, f32[400,128]{1,0:T(8,128)}, u32[]{:S(2)}) copy-start(f32[400,128]{1,0:T(8,128)} %r_in.3) | copy-start | bytes 614404
  56.4 6.9 %copy-start.4 = (f32[400,128]{1,0:T(8,128)S(1)}, f32[400,128]{1,0:T(8,128)}, u32[]{:S(2)}) copy-start(f32[400,128]{1,0:T(8,128)} %param.15) | copy-start | bytes 614404
